TPU v7x, 256 devices: a whole 4x4x8 slice. The times are simulated.
256 devices in a mesh: gx: 16 (over x, y), gy: 16 (over z, core).
Axes of the slice: x: 4, y: 4, z: 8, core: 2. Of those that a mesh axis runs over, the one named last changes fastest.
Arguments:
- snapshots: bfloat16 [3, 1024, 1024, 256], P(None, 'gx', 'gy'), may hold values from -70 to 70
- prior: float32 [256, 256], replicated, may hold values from -0.15 to 0.5, as said below
Outputs:
- modes: float32 [3, 512, 512, 256], P(None, 'gx', 'gy')
- factor: float32 [256, 256], replicated
Inputs may be any that keep to these rules, and one draw needn't show every extreme that they name: `prior`: upper triangular with a positive diagonal.
All inputs are finite; a program needn't handle non-finite values.
Results may differ from a plain program's by a relative error of at most 0.008.
Values may be sent and summed in bfloat16 or wider, within the bound.
A program may use at most 320 MiB of HBM per device.

v0:
```python
import jax
import jax.numpy as jnp
from jax import lax
from jax.sharding import PartitionSpec as P

filter_taps = (
    1.0 / 256,
    8.0 / 256,
    28.0 / 256,
    56.0 / 256,
    70.0 / 256,
    56.0 / 256,
    28.0 / 256,
    8.0 / 256,
    1.0 / 256,
)


def padded_2(block, sides, width):
    for axis, dim in sides:
        count = lax.axis_size(axis)
        forward = [(i, i + 1) for i in range(count - 1)]
        forward.append((count - 1, 0))
        backward = [(target, source) for source, target in forward]
        low = lax.ppermute(
            lax.slice_in_dim(block, block.shape[dim] - width, None, axis=dim), axis, forward
        )
        high = lax.ppermute(lax.slice_in_dim(block, 0, width, axis=dim), axis, backward)
        block = jnp.concatenate([low, block, high], axis=dim)
    return block


def pass_along(padded, along, coarse_count):
    columns = padded.shape[3]
    if along == 2:
        paired = padded.reshape(padded.shape[0], padded.shape[1], coarse_count + 4, 2 * columns)
    else:
        paired = padded.reshape(padded.shape[0], coarse_count + 4, 2, padded.shape[2], columns)
    result = None
    for offset in range(9):
        start = offset // 2
        parity = offset % 2
        if along == 2:
            picked = paired[
                :, :, start : start + coarse_count, parity * columns : (parity + 1) * columns
            ]
        else:
            picked = paired[:, start : start + coarse_count, parity]
        term = filter_taps[offset] * picked.astype(jnp.float32)
        result = term if result is None else result + term
    return result


def factorize(gram_matrix):
    width = gram_matrix.shape[0]
    positions = jnp.arange(width, dtype=jnp.int32)
    lower_start = jnp.zeros((width, width), jnp.float32)
    inverse_start = jnp.zeros((width, width), jnp.float32)

    def one_column(index, carry):
        lower_now, inverse_now = carry
        picked = (positions == index).astype(jnp.float32)
        lower_row = jnp.dot(picked, lower_now, precision=lax.Precision.HIGHEST)
        target = jnp.dot(gram_matrix, picked, precision=lax.Precision.HIGHEST)
        column = target - jnp.dot(lower_now, lower_row, precision=lax.Precision.HIGHEST)
        pivot = jnp.sqrt(jnp.sum(column * picked))
        column = jnp.where(positions >= index, column / pivot, 0.0)
        lower_now = lower_now + column[:, None] * picked[None, :]
        full_row = lower_row + pivot * picked
        inverse_row = (
            picked - jnp.dot(full_row, inverse_now, precision=lax.Precision.HIGHEST)
        ) / pivot
        inverse_now = inverse_now + picked[:, None] * inverse_row[None, :]
        return (lower_now, inverse_now)

    lower_done, inverse_done = lax.fori_loop(0, width, one_column, (lower_start, inverse_start))
    return (lower_done.T, inverse_done.T)


def shards(snapshots, prior):
    width_x = snapshots.shape[1]
    width_y = snapshots.shape[2]
    columns = snapshots.shape[3]
    devices = lax.axis_size("gx") * lax.axis_size("gy")
    row_count = 3 * (width_x // 2) * (width_y // 2) * devices
    padded = padded_2(snapshots, (("gx", 1), ("gy", 2)), 4)
    halved = lax.optimization_barrier(pass_along(padded, 2, width_y // 2).astype(jnp.bfloat16))
    coarse = pass_along(halved, 1, width_x // 2)
    coarse_rows = coarse.reshape(-1, columns)
    gram_local = jnp.dot(coarse_rows.T, coarse_rows, precision=lax.Precision.HIGHEST)
    prior_gram = jnp.dot(prior.T, prior, precision=lax.Precision.HIGHEST)
    gram_total = lax.psum(gram_local, ("gx", "gy"))
    upper_factor, inverse_upper = factorize(gram_total / row_count + prior_gram)
    modes = jnp.dot(coarse_rows, inverse_upper, precision=lax.Precision.HIGHEST).reshape(
        coarse.shape
    )
    return (modes, upper_factor)


def solution(mesh):
    placed = (P(None, "gx", "gy", None), P())
    return jax.shard_map(
        shards,
        mesh=mesh,
        in_specs=placed,
        out_specs=(P(None, "gx", "gy", None), P()),
        check_vma=False,
    )
```

profile of v0, /device:TPU:1, one launch (start us, length us, event | category | flops | bytes accessed | tf_op | source)
XLA Modules:
  0.0 1018.4 jit_solution(14221286541785110788)
XLA Ops:
  7.2 1.2 fusion.27
  8.4 2.2 collective-permute-start
  10.6 3.7 collective-permute-start.1
  14.4 6.4 copy.12
  22.3 4.7 collective-permute-start.2
  27.1 5.2 collective-permute-done.2
  32.3 2.8 collective-permute-done.3
  35.1 7.1 pad_maximum_fusion
  42.2 4.7 copy.14
  46.9 12.7 %reshape.76 = bf16[3,72,36,512]{3,2,1,0:T(8,128)(2,1)} reshape(bf16[3,72,72,256]{3,2,1,0:T(8,128)(2,1)} %copy.14) | data formatting | bytes 15925248 | tf_op jit(solution)/shard_map/reshape | solution.py:36
  59.6 18.3 %add_convert_fusion = bf16[3,72,32,256]{3,2,1,0:T(8,128)(2,1)S(1)} fusion(bf16[3,72,36,512]{3,2,1,0:T(8,128)(2,1)} %reshape.76), kind=kLoop, calls=%fused_computation.26 | loop fusion | flops 47775744 | bytes 35389440 | tf_op jit(solution)/shard_map/convert_element_type | solution.py:87
  78.0 3.5 add_add_fusion
  81.4 1.6 copy-done.1
  83.1 5.8 fusion.23
  88.9 250.2 %all-reduce.2.cloned.1.call-done = f32[256,256]{1,0:T(8,128)} async-done(((f32[256,256]{1,0:T(8,128)}), f32[256,256]{1,0:T(8,128)}) %all-reduce.2.cloned.1.call-update) | async-done | bytes 262160 | tf_op jit(solution)/shard_map/psum | solution.py:92
  339.1 1.5 convolution_add_fusion
  340.7 663.8 %while.17 = (s32[]{:T(128)}, f32[256,256]{1,0:T(8,128)S(1)}, f32[256,256]{1,0:T(8,128)S(1)}, f32[256,256]{1,0:T(8,128)S(1)}, s32[]{:T(128)}, /*index=5*/s32[]{:T(128)}) while((s32[]{:T(128)}, f32[256,256]{1,0:T(8,128)S(1)}, f32[256,256]{1,0:T(8,128)S(1)}, f32[256,256]{1,0:T(8,128)S(1)}, s32[]{:T(128)}, ...), condition=%wide.region_3.4_spmd.clone.clone, body=%wide.region_1.3_spmd.clone.clone.sunk | while | flops 3739906 | bytes 2118010 | solution.py:76
  344.1 0.7 select_reduce_fusion.2
  346.7 0.7 select_reduce_fusion.2
  349.3 0.7 select_reduce_fusion.2
  351.9 0.7 select_reduce_fusion.2
  354.5 0.7 select_reduce_fusion.2
  357.0 0.7 select_reduce_fusion.2
  359.6 0.7 select_reduce_fusion.2
  362.2 0.7 select_reduce_fusion.2
  370.0 0.7 select_reduce_fusion.2
  372.6 0.7 select_reduce_fusion.2
  375.2 0.7 select_reduce_fusion.2
  377.8 0.7 select_reduce_fusion.2
  380.4 0.7 select_reduce_fusion.2
  383.0 0.7 select_reduce_fusion.2
  385.6 0.7 select_reduce_fusion.2
  393.4 0.7 select_reduce_fusion.2
  395.9 0.7 select_reduce_fusion.2
  398.5 0.7 select_reduce_fusion.2
  401.1 0.7 select_reduce_fusion.2
  403.7 0.7 select_reduce_fusion.2
  406.3 0.7 select_reduce_fusion.2
  408.9 0.7 select_reduce_fusion.2
  411.5 0.7 select_reduce_fusion.2
  419.3 0.7 select_reduce_fusion.2
  421.9 0.7 select_reduce_fusion.2
  424.5 0.7 select_reduce_fusion.2
  427.1 0.7 select_reduce_fusion.2
  429.7 0.7 select_reduce_fusion.2
  432.3 0.7 select_reduce_fusion.2
  434.8 0.7 select_reduce_fusion.2
  442.6 0.7 select_reduce_fusion.2
  445.2 0.7 select_reduce_fusion.2
  447.8 0.7 select_reduce_fusion.2
  450.4 0.7 select_reduce_fusion.2
  453.0 0.7 select_reduce_fusion.2
  455.6 0.7 select_reduce_fusion.2
  458.2 0.7 select_reduce_fusion.2
  460.8 0.7 select_reduce_fusion.2
  468.6 0.7 select_reduce_fusion.2
  471.1 0.7 select_reduce_fusion.2
  473.7 0.7 select_reduce_fusion.2
  476.3 0.7 select_reduce_fusion.2
  478.9 0.7 select_reduce_fusion.2
  481.5 0.7 select_reduce_fusion.2
  484.1 0.7 select_reduce_fusion.2
  1004.5 6.2 fusion.21
  1010.7 0.8 copy.15
  (2784 shorter events, 442.3 us)
Async XLA Ops:
  7.2 332.0 %copy-start = (f32[256,256]{1,0:T(8,128)S(1)}, f32[256,256]{1,0:T(8,128)}, u32[]{:S(2)}) copy-start(f32[256,256]{1,0:T(8,128)} %param.5) | copy-start | bytes 786436
  7.2 332.0 %all-reduce.2.cloned.1.call-start = ((), (), s32[]{:S(2)}) async-start(), calls=%async_computation | async-start | bytes 524288 | tf_op jit(solution)/shard_map/psum | solution.py:92
  8.4 12.7 %collective-permute-start = (bf16[3,4,64,256]{3,2,1,0:T(8,128)(2,1)S(1)}, bf16[3,4,64,256]{3,2,1,0:T(8,128)(2,1)S(1)}, u32[]{:S(2)}, u32[]{:S(2)}) collective-permute-start(bf16[3,4,64,256]{3,2,1,0:T(8,128)(2,1)S(1)} %get-tuple-element.149), channel_id=1, source_target_pairs={{0,16},{16,32},{32,48},{48,64},{64,80},{80,96},{96,112},{112,128},... | collective-permute-start | bytes 1179656 | tf_op jit(solution)/shard_map/ppermute | solution.py:25
  10.6 10.8 %collective-permute-start.1 = (bf16[3,4,64,256]{3,2,1,0:T(8,128)(2,1)S(1)}, bf16[3,4,64,256]{3,2,1,0:T(8,128)(2,1)S(1)}, u32[]{:S(2)}, u32[]{:S(2)}) collective-permute-start(bf16[3,4,64,256]{3,2,1,0:T(8,128)(2,1)S(1)} %get-tuple-element.150), channel_id=1, source_target_pairs={{16,0},{32,16},{48,32},{64,48},{80,64},{96,80},{112,96},{128,112},... | collective-permute-start | bytes 1179656 | tf_op jit(solution)/shard_map/ppermute | solution.py:28
  22.3 10.0 collective-permute-start.2
  27.1 8.0 collective-permute-start.3
  81.4 1.6 copy-start.1
Sparse Core Ops, SparseCore 0:
  89.0 250.0 all-reduce.1
where the time goes:
time: 1020 us
  waiting for transfers between devices  259 us (25%)
  matrix products  258 us (25%)
  other arithmetic  254 us (25%)
  loops' own time  194 us (19%)
  local copies, waits for them, and re-layouts  29.9 us (3%)
  between operations  14.1 us (1%)
  starting transfers between devices  10.7 us (1%)
    psum x1, waiting for transfers between devices, shards(): gram_total = lax.psum(gram_local, ('gx', 'gy'))  250 us
    another operation x1, loops' own time, factorize(): lax.fori_loop(0, width, one_column, (lower_start, inverse_start))  194 us
    reduce_sum x256, other arithmetic, one_column(): pivot = jnp.sqrt(jnp.sum(column * picked))  168 us
    dot_general x256, matrix products, one_column(): jnp.dot(lower_now, lower_row, precision=lax.Precision.HIGHEST)  72.4 us
    dot_general x256, matrix products, one_column(): target = jnp.dot(gram_matrix, picked, precision=lax.Precision.HIGHEST)  69 us
    dot_general x256, matrix products, one_column(): lower_row = jnp.dot(picked, lower_now, precision=lax.Precision.HIGHEST)  53.6 us
    dot_general x256, matrix products, one_column(): jnp.dot(full_row, inverse_now, precision=lax.Precision.HIGHEST)  49.3 us
    add x256, other arithmetic, one_column(): inverse_now = inverse_now + picked[:, None] * inverse_row[None, :]  41.6 us
  transfers between devices with their start and end apart: 5, of which 4 were waited for; matrix products, arithmetic and copies ran while one was open for 1% of the time, Pallas kernels for 0%

commit v1 on v0

v1 whole, which is shorter than its diff:
```python
import jax
import jax.numpy as jnp
from jax import lax
from jax.experimental import pallas as pl
from jax.experimental.pallas import tpu as pltpu
from jax.sharding import PartitionSpec as P

f32 = jnp.float32
bf16 = jnp.bfloat16
MESH = pl.DeviceIdType.MESH
TAPS = (1, 8, 28, 56, 70, 56, 28, 8, 1)
RING = 16
PARTS = 3
FINE = 64
HALF = 32
K = 256
LANES = 128
ROWS = 40
GROUP = 4
SLOTS = 40
CHUNK = 24
PANEL = 16


def y_matrix():
    shape = (GROUP * ROWS, GROUP * FINE)
    row = lax.broadcasted_iota(jnp.int32, shape, 0)
    column = lax.broadcasted_iota(jnp.int32, shape, 1)
    slab = row // ROWS
    index = row % ROWS
    cell = jnp.where(index < HALF, index, jnp.where(index < HALF + 2, index - HALF - 2, index - 2))
    offset = column % FINE - 2 * cell + 4
    offset = jnp.where((slab == column // FINE) & (index < HALF + 4), offset, -1)
    taps = jnp.zeros(shape, f32)
    for place, tap in enumerate(TAPS):
        taps = jnp.where(offset == place, tap / 65536.0, taps)
    return jnp.where(slab % 2 == 1, 8.0 * taps, taps).astype(bf16)


def x_sum(load, cell):
    total = None

    def pair(first, second, low, high):
        have = [load(2 * q + second) for q in (low, high) if 0 <= q < HALF]
        if not have:
            return None
        value = have[0] if len(have) == 1 else have[0] + have[1]
        return value if first == 1.0 else first * value

    terms = [
        pair(1.0, 0, cell - 2, cell + 2),
        pair(28.0, 0, cell - 1, cell + 1),
        pair(70.0, 0, cell, -1),
        pair(1.0, 1, cell - 2, cell + 1),
        pair(7.0, 1, cell - 1, cell),
    ]
    for term in terms:
        if term is not None:
            total = term if total is None else total + term
    return total


def filter_kernel(
    snap_ref,
    prior_ref,
    coarse_ref,
    gram_ref,
    tile,
    prior_tile,
    ysum,
    edge,
    coarse,
    rounded,
    x_out,
    x_in,
    y_out,
    y_in,
    c_out,
    c_in,
    packed,
    prior_gram,
    rs_in,
    gy_in,
    ag_in,
    load_sem,
    store_sem,
    halo_send,
    halo_recv,
    rs_send,
    rs_recv,
    gy_send,
    gy_recv,
    ag_send,
    ag_recv,
):
    gx = lax.axis_index("gx")
    gy = lax.axis_index("gy")
    gx_next, gx_last = lax.rem(gx + 1, RING), lax.rem(gx + RING - 1, RING)
    gy_next, gy_last = lax.rem(gy + 1, RING), lax.rem(gy + RING - 1, RING)

    slabs = 16
    loads = []
    for m in range(PARTS):
        for q in range(FINE // slabs):
            place = (m, pl.ds(q * slabs, slabs))
            loads.append(
                pltpu.make_async_copy(
                    snap_ref.at[place], tile.at[place], load_sem.at[len(loads)]
                )
            )
    load_prior = pltpu.make_async_copy(prior_ref, prior_tile, load_sem.at[len(loads)])
    for load in loads:
        load.start()
    load_prior.start()

    barrier = pltpu.get_barrier_semaphore()

    def greet(step, carry):
        pl.semaphore_signal(
            barrier, inc=1, device_id=(lax.rem(gx + step, RING), gy), device_id_type=MESH
        )
        pl.semaphore_signal(
            barrier, inc=1, device_id=(gx, lax.rem(gy + step, RING)), device_id_type=MESH
        )
        return carry

    lax.fori_loop(1, RING, greet, 0)
    for ox in (gx_last, gx_next):
        for oy in (gy_last, gy_next):
            pl.semaphore_signal(barrier, inc=1, device_id=(ox, oy), device_id_type=MESH)

    taps = y_matrix()
    for m in range(PARTS):
        for q in range(FINE // slabs):
            loads[m * (FINE // slabs) + q].wait()

            def y_group(g, carry, m=m, q=q):
                first = q * slabs + g * GROUP
                fine = tile[m, pl.ds(first, GROUP)].reshape(GROUP * FINE, K)
                sums = jnp.dot(taps, fine, preferred_element_type=f32)
                ysum[m, pl.ds(first, GROUP)] = sums.reshape(GROUP, ROWS, K)
                return carry

            lax.fori_loop(0, slabs // GROUP, y_group, 0, unroll=True)

    for m in range(PARTS):
        for side in range(2):
            for step in range(2):
                cell = (-2, HALF)[side] + step
                value = x_sum(lambda x: ysum[m, x, pl.ds(0, HALF), :], cell)
                x_out[side, m, step] = value.astype(bf16)

    def edge_part(m, carry):
        for slot in range(HALF + 4):
            cell = slot if slot < HALF else (slot - HALF - 2 if slot < HALF + 2 else slot - 2)
            value = x_sum(lambda x: ysum[m, x, pl.ds(HALF, 8), :], cell)
            rows = pl.ds(pl.multiple_of(m * (SLOTS * 8) + slot * 8, 8), 8)
            edge[0, rows, :] = value[:, :LANES]
            edge[1, rows, :] = value[:, LANES:]
        for slot in range(HALF + 4, SLOTS):
            rows = pl.ds(pl.multiple_of(m * (SLOTS * 8) + slot * 8, 8), 8)
            edge[:, rows, :] = jnp.zeros((2, 8, LANES), f32)
        return carry

    pl.semaphore_wait(barrier, 2 * (RING - 1) + 4)
    halos = []

    def send(source, target, peer):
        copy = pltpu.make_async_remote_copy(
            src_ref=source,
            dst_ref=target,
            send_sem=halo_send.at[len(halos)],
            recv_sem=halo_recv.at[len(halos)],
            device_id=peer,
            device_id_type=MESH,
        )
        copy.start()
        halos.append(copy)

    send(x_out.at[0], x_in.at[0], (gx_last, gy))
    send(x_out.at[1], x_in.at[1], (gx_next, gy))

    lax.fori_loop(0, PARTS, edge_part, 0)
    for side in range(2):
        for m in range(PARTS):
            outer = []
            for step in range(2):
                start = m * SLOTS * 8 + side * 2 + step
                picked = jnp.concatenate(
                    [edge[h, pl.ds(start, SLOTS, stride=8), :] for h in range(2)], axis=1
                )
                y_out[side, m, step] = picked[:HALF].astype(bf16)
                outer.append(picked[HALF:])
            c_out[side, pl.ds(m * 16, 16), :] = jnp.concatenate(outer, axis=0).astype(bf16)
    send(y_out.at[0], y_in.at[0], (gx, gy_last))
    send(y_out.at[1], y_in.at[1], (gx, gy_next))
    for side, oy in ((0, gy_last), (1, gy_next)):
        for other, ox in ((0, gx_last), (1, gx_next)):
            send(c_out.at[side], c_in.at[side, other], (ox, oy))

    def inside(step, carry):
        m = step // 4
        row = pl.multiple_of(lax.rem(step, 4) * 8, 8)
        for cell in range(HALF):
            value = x_sum(lambda x: ysum[m, x, pl.ds(row, 8), :], cell)
            rows = pl.ds(pl.multiple_of(m * (HALF * HALF) + cell * HALF + row, 8), 8)
            coarse[0, rows, :] = value[:, :LANES]
            coarse[1, rows, :] = value[:, LANES:]
        return carry

    lax.fori_loop(0, PARTS * 4, inside, 0)

    load_prior.wait()
    half = K // 2
    squared = lax.dot_general(
        prior_tile[...],
        prior_tile[...],
        (((0,), (0,)), ((), ())),
        precision=lax.Precision.HIGHEST,
        preferred_element_type=f32,
    )
    prior_gram[0:half, :] = squared[:half, :half]
    prior_gram[half:K, :] = squared[:half, half:]
    prior_gram[K : K + half, :] = squared[half:, half:]

    for copy in halos:
        copy.wait()
    for m in range(PARTS):
        for side in range(2):
            for step in range(2):
                cell = (HALF - 2, 0)[side] + step
                rows = pl.ds(m * HALF * HALF + cell * HALF, HALF)
                value = x_in[side, m, step].astype(f32)
                for h in range(2):
                    coarse[h, rows, :] += value[:, h * LANES : (h + 1) * LANES]
    for m in range(PARTS):
        for side in range(2):
            for step in range(2):
                cell = (HALF - 2, 0)[side] + step
                rows = pl.ds(m * HALF * HALF + cell, HALF, stride=HALF)
                value = y_in[side, m, step].astype(f32)
                for h in range(2):
                    coarse[h, rows, :] += value[:, h * LANES : (h + 1) * LANES]
    for side in range(2):
        for other in range(2):
            corner = c_in[side, other].astype(f32)
            for m in range(PARTS):
                for step in range(2):
                    column = (HALF - 2, 0)[side] + step
                    for along in range(2):
                        row = (HALF - 2, 0)[other] + along
                        source = (m * 2 + step) * 8 + other * 2 + along
                        target = m * HALF * HALF + row * HALF + column
                        value = corner[source : source + 1, :]
                        for h in range(2):
                            lanes = value[:, h * LANES : (h + 1) * LANES]
                            coarse[h, target : target + 1, :] += lanes

    packed[...] = jnp.zeros(packed.shape, f32)
    block = 512

    def cross(step, carry):
        rows = pl.ds(pl.multiple_of(step * block, block), block)
        part = jnp.concatenate([coarse[h, rows, :] for h in range(2)], axis=1).astype(bf16)
        rounded[rows, :] = part
        contract = (((0,), (0,)), ((), ()))
        top = lax.dot_general(part[:, :half], part, contract, preferred_element_type=f32)
        low = lax.dot_general(part[:, half:], part[:, half:], contract, preferred_element_type=f32)
        sums = jnp.concatenate([top[:, :half], top[:, half:], low], axis=0)
        packed[...] += sums.reshape(packed.shape)
        return carry

    lax.fori_loop(0, PARTS * HALF * HALF // block, cross, 0)
    store = pltpu.make_async_copy(rounded, coarse_ref, store_sem)
    store.start()

    def exchange(source_of, target, send_sem, recv_sem, along, me):
        copies = []
        for step in range(1, RING):
            peer = lax.rem(me + step, RING)
            copies.append(
                pltpu.make_async_remote_copy(
                    src_ref=source_of(peer),
                    dst_ref=target.at[me],
                    send_sem=send_sem.at[step],
                    recv_sem=recv_sem.at[step],
                    device_id=(peer, gy) if along == 0 else (gx, peer),
                    device_id_type=MESH,
                )
            )
        for copy in copies:
            copy.start()
        for copy in copies:
            copy.wait()

    def sum_slots(slots):
        total = slots[0]
        for slot in range(1, RING):
            total = total + slots[slot]
        return total

    rs_in[gx] = packed[gx]
    exchange(lambda peer: packed.at[peer], rs_in, rs_send, rs_recv, 0, gx)
    gy_in[gy] = sum_slots(rs_in)
    exchange(lambda peer: gy_in.at[gy], gy_in, gy_send, gy_recv, 1, gy)
    ag_in[gx] = sum_slots(gy_in)
    exchange(lambda peer: ag_in.at[gx], ag_in, ag_send, ag_recv, 0, gx)

    count = PARTS * HALF * HALF * RING * RING
    gram_ref[...] = ag_in[...].reshape(gram_ref.shape) * (1.0 / count) + prior_gram[...]
    store.wait()


def filter_call(snapshots, prior):
    rows = PARTS * HALF * HALF
    vmem = pltpu.VMEM
    dma = pltpu.SemaphoreType.DMA
    return pl.pallas_call(
        filter_kernel,
        out_shape=(
            jax.ShapeDtypeStruct((rows, K), bf16),
            jax.ShapeDtypeStruct((K + K // 2, K // 2), f32),
        ),
        in_specs=[pl.BlockSpec(memory_space=pl.ANY)] * 2,
        out_specs=(pl.BlockSpec(memory_space=pl.ANY), pl.BlockSpec(memory_space=pltpu.VMEM)),
        scratch_shapes=[
            vmem((PARTS, FINE, FINE, K), bf16),
            vmem((K, K), f32),
            vmem((PARTS, FINE, ROWS, K), f32),
            vmem((2, PARTS * SLOTS * 8, LANES), f32),
            vmem((2, rows, LANES), f32),
            vmem((rows, K), bf16),
            vmem((2, PARTS, 2, HALF, K), bf16),
            vmem((2, PARTS, 2, HALF, K), bf16),
            vmem((2, PARTS, 2, HALF, K), bf16),
            vmem((2, PARTS, 2, HALF, K), bf16),
            vmem((2, PARTS * 16, K), bf16),
            vmem((2, 2, PARTS * 16, K), bf16),
            vmem((RING, CHUNK, K // 2), f32),
            vmem((K + K // 2, K // 2), f32),
            vmem((RING, CHUNK, K // 2), f32),
            vmem((RING, CHUNK, K // 2), f32),
            vmem((RING, CHUNK, K // 2), f32),
            dma((13,)),
            dma,
            dma((8,)),
            dma((8,)),
            dma((RING,)),
            dma((RING,)),
            dma((RING,)),
            dma((RING,)),
            dma((RING,)),
            dma((RING,)),
        ],
        compiler_params=pltpu.CompilerParams(
            collective_id=0, has_side_effects=True, vmem_limit_bytes=48 * 2**20
        ),
        name="filter_and_gram",
    )(snapshots, prior)


def split(value):
    high = value.astype(bf16)
    rest = value - high.astype(f32)
    middle = rest.astype(bf16)
    return high, middle, (rest - middle.astype(f32)).astype(bf16)


def factor_panels(work, upper, inverse):
    below = lax.broadcasted_iota(jnp.int32, (PANEL, 128), 0)
    for first in range(0, K, PANEL):
        rows = pl.ds(first, PANEL)
        strip = work[rows, :]
        columns = [
            jnp.broadcast_to(strip[:, first + k : first + k + 1], (PANEL, 128))
            for k in range(PANEL)
        ]
        tiles = [strip[:, t : t + 128] for t in range(0, 2 * K, 128)]
        pivots = jnp.zeros((PANEL, 128), f32)
        for j in range(PANEL):
            pivot = jnp.broadcast_to(columns[j][j : j + 1, :], (PANEL, 128))
            pivots = jnp.where(below == j, pivot, pivots)
            if j == PANEL - 1:
                break
            factor = jnp.where(below > j, columns[j] / pivot, 0.0)
            for k in range(j + 1, PANEL):
                columns[k] -= factor * jnp.broadcast_to(columns[k][j : j + 1, :], (PANEL, 128))
            tiles = [t - factor * jnp.broadcast_to(t[j : j + 1, :], (PANEL, 128)) for t in tiles]
        scale = lax.rsqrt(pivots)
        strip = jnp.concatenate([t * scale for t in tiles], axis=1)
        upper[rows, :] = strip[:, :K]
        inverse[rows, :] = strip[:, K:]
        done = first + PANEL
        if done < K:
            high, middle, low = split(strip)
            left = jnp.concatenate([high, high, middle, high, low, middle], axis=0)
            right = jnp.concatenate([high, middle, high, low, high, middle], axis=0)
            work[done:, :] -= lax.dot_general(
                left[:, done:K], right, (((0,), (0,)), ((), ())), preferred_element_type=f32
            )


def factor_kernel(
    coarse_ref, gram_ref, modes_ref, upper_ref, rows_in, work, upper, inverse, out, load_sem, store_sem
):
    load = pltpu.make_async_copy(coarse_ref, rows_in, load_sem)
    load.start()
    row = lax.broadcasted_iota(jnp.int32, (K, K), 0)
    column = lax.broadcasted_iota(jnp.int32, (K, K), 1)
    half = K // 2
    work[:half, :half] = gram_ref[:half, :]
    work[:half, half:K] = gram_ref[half:K, :]
    work[half:, :half] = jnp.zeros((half, half), f32)
    work[half:, half:K] = gram_ref[K:, :]
    work[:, K:] = jnp.where(row == column, 1.0, 0.0)
    factor_panels(work, upper, inverse)
    upper_ref[...] = jnp.where(row <= column, upper[...], 0.0)
    high, middle, low = split(inverse[...].T)
    load.wait()
    count = rows_in.shape[0]
    block = 512
    stores = []
    for step in range(count // block):
        rows = pl.ds(step * block, block)
        part = rows_in[rows, :]
        value = jnp.dot(part, high, preferred_element_type=f32)
        value += jnp.dot(part, middle, preferred_element_type=f32)
        out[rows, :] = value
        stores.append(
            pltpu.make_async_copy(out.at[rows], modes_ref.at[rows], store_sem.at[step])
        )
        stores[-1].start()
    for store in stores:
        store.wait()


def factor_call(coarse, gram):
    rows = coarse.shape[0]
    vmem = pltpu.VMEM
    return pl.pallas_call(
        factor_kernel,
        out_shape=(jax.ShapeDtypeStruct((rows, K), f32), jax.ShapeDtypeStruct((K, K), f32)),
        in_specs=[pl.BlockSpec(memory_space=pl.ANY), pl.BlockSpec(memory_space=pltpu.VMEM)],
        out_specs=(pl.BlockSpec(memory_space=pl.ANY), pl.BlockSpec(memory_space=pltpu.VMEM)),
        scratch_shapes=[
            vmem((rows, K), bf16),
            vmem((K, 2 * K), f32),
            vmem((K, K), f32),
            vmem((K, K), f32),
            vmem((rows, K), f32),
            pltpu.SemaphoreType.DMA,
            pltpu.SemaphoreType.DMA((rows // 512,)),
        ],
        compiler_params=pltpu.CompilerParams(vmem_limit_bytes=48 * 2**20),
        name="factor_and_modes",
    )(coarse, gram)


def shards(snapshots, prior):
    coarse, gram = filter_call(snapshots, prior)
    modes, upper = factor_call(coarse, gram)
    return (modes.reshape(PARTS, HALF, HALF, K), upper)


def solution(mesh):
    return jax.shard_map(
        shards,
        mesh=mesh,
        in_specs=(P(None, "gx", "gy", None), P()),
        out_specs=(P(None, "gx", "gy", None), P()),
        check_vma=False,
    )
```

time: 1020 us -> 50.9 us (0.05)
  waiting for transfers between devices: 259 us -> 0 us
  matrix products: 258 us -> 0 us
  other arithmetic: 254 us -> 0 us
  loops' own time: 194 us -> 0 us
  Pallas kernels: 0 us -> 49.1 us
  local copies, waits for them, and re-layouts: 29.9 us -> 0.94 us
  between operations: 14.1 us -> 0.65 us
  starting transfers between devices: 10.7 us -> 0 us
    dot_general x1027 -> x0, matrix products: 258 us -> none  [the longest x256 72.4 us: one_column(): jnp.dot(lower_now, lower_row, precision=lax.Precision.HIGHEST)]
    psum x1 -> x0, waiting for transfers between devices: 250 us -> none  [shards(): gram_total = lax.psum(gram_local, ('gx', 'gy'))]
    another operation x1 -> x0, loops' own time: 194 us -> none  [factorize(): lax.fori_loop(0, width, one_column, (lower_start, inverse_start))]
    reduce_sum x256 -> x0, other arithmetic: 168 us -> none  [one_column(): pivot = jnp.sqrt(jnp.sum(column * picked))]
    pallas_call x0 -> x2, Pallas kernels: none -> 49.1 us  [the longest x1 38 us: filter_call(): pl.pallas_call(filter_kernel, out_shape=(jax.ShapeDtypeStruct((rows, K),...]
    add x513 -> x0, other arithmetic: 46.4 us -> none  [the longest x256 41.6 us: one_column(): inverse_now = inverse_now + picked[:, None] * inverse_row[None, :]]
    convert_element_type x257 -> x0, other arithmetic: 19.3 us -> none  [the longest x1 18.3 us: shards(): pass_along(padded, 2, width_y // 2).astype(jnp.bfloat16)]
    reshape x1 -> x0, local copies, waits for them, and re-layouts: 12.7 us -> none  [pass_along(): padded.reshape(padded.shape[0], padded.shape[1], coarse_count + 4, 2 * co...]
  transfers between devices with their start and end apart: 5 -> 0, of which waited for: 4 -> 0; matrix products, arithmetic and copies ran while one was open for 1% -> 0% of each run, Pallas kernels for 0% -> 0%
where the time goes in v1:
time: 50.9 us; the launch traced here: 50.7 us
  Pallas kernels  49.1 us (96%)
  local copies, waits for them, and re-layouts  0.94 us (2%)
  between operations  0.65 us (1%)
    pallas_call x1, Pallas kernels, filter_call(): pl.pallas_call(filter_kernel, out_shape=(jax.ShapeDtypeStruct((rows, K),...  38 us
    pallas_call x1, Pallas kernels, factor_call(): pl.pallas_call(factor_kernel, out_shape=(jax.ShapeDtypeStruct((rows, K),...  11 us

profile of v1, /device:TPU:1, one launch (start us, length us, event | category | flops | bytes accessed | tf_op | source)
XLA Modules:
  0.0 50.7 jit_solution(286277440068875591)
XLA Ops:
  0.6 0.0 copy-start
  0.6 0.9 %copy-done = f32[256,256]{1,0:T(8,128)S(1)} copy-done((f32[256,256]{1,0:T(8,128)S(1)}, f32[256,256]{1,0:T(8,128)}, u32[]{:S(2)}) %copy-start) | copy-done | bytes 262168
  1.6 38.0 %filter_and_gram.1 = (bf16[3072,256]{1,0:T(8,128)(2,1)S(1)}, f32[384,128]{1,0:T(8,128)S(1)}) custom-call(bf16[3,64,64,256]{3,2,1,0:T(8,128)(2,1)} %snap_ref.1, f32[256,256]{1,0:T(8,128)S(1)} %copy-done), custom_call_target="tpu_custom_call" | custom-call | tf_op jit(solution)/shard_map/filter_and_gram/pallas_call | solution.py:318
  39.6 11.0 %factor_and_modes.1 = (f32[3072,256]{1,0:T(8,128)}, f32[256,256]{1,0:T(8,128)}) custom-call(bf16[3072,256]{1,0:T(8,128)(2,1)S(1)} %get-tuple-element.6.coarse_ref, f32[384,128]{1,0:T(8,128)S(1)} %get-tuple-element.7.gram_ref), custom_call_target="tpu_custom_call" | custom-call | tf_op jit(solution)/shard_map/factor_and_modes/pallas_call | solution.py:440
Async XLA Ops:
  0.6 1.0 %copy-start = (f32[256,256]{1,0:T(8,128)S(1)}, f32[256,256]{1,0:T(8,128)}, u32[]{:S(2)}) copy-start(f32[256,256]{1,0:T(8,128)} %prior_ref.1) | copy-start | bytes 786436

commit v2 on v1

v2 whole, which is shorter than its diff:
```python
import jax
import jax.numpy as jnp
from jax import lax
from jax.experimental import pallas as pl
from jax.experimental.pallas import tpu as pltpu
from jax.sharding import PartitionSpec as P

f32 = jnp.float32
bf16 = jnp.bfloat16
MESH = pl.DeviceIdType.MESH
TAPS = (1, 8, 28, 56, 70, 56, 28, 8, 1)
RING = 16
PARTS = 3
FINE = 64
HALF = 32
K = 256
LANES = 128
ROWS = 40
GROUP = 4
SLOTS = 40
DEEP = 8
MEMBERS = 32
PANEL = 16


def y_matrix():
    shape = (GROUP * ROWS, GROUP * FINE)
    row = lax.broadcasted_iota(jnp.int32, shape, 0)
    column = lax.broadcasted_iota(jnp.int32, shape, 1)
    slab = row // ROWS
    index = row % ROWS
    cell = jnp.where(index < HALF, index, jnp.where(index < HALF + 2, index - HALF - 2, index - 2))
    offset = column % FINE - 2 * cell + 4
    offset = jnp.where((slab == column // FINE) & (index < HALF + 4), offset, -1)
    taps = jnp.zeros(shape, f32)
    for place, tap in enumerate(TAPS):
        taps = jnp.where(offset == place, tap / 65536.0, taps)
    return jnp.where(slab % 2 == 1, 8.0 * taps, taps).astype(bf16)


def x_sum(load, cell):
    total = None

    def pair(first, second, low, high):
        have = [load(2 * q + second) for q in (low, high) if 0 <= q < HALF]
        if not have:
            return None
        value = have[0] if len(have) == 1 else have[0] + have[1]
        return value if first == 1.0 else first * value

    terms = [
        pair(1.0, 0, cell - 2, cell + 2),
        pair(28.0, 0, cell - 1, cell + 1),
        pair(70.0, 0, cell, -1),
        pair(1.0, 1, cell - 2, cell + 1),
        pair(7.0, 1, cell - 1, cell),
    ]
    for term in terms:
        if term is not None:
            total = term if total is None else total + term
    return total


def x_cell(slot):
    return slot if slot < HALF else (slot - HALF - 2 if slot < HALF + 2 else slot - 2)


def cross(left, right):
    contract = (((0,), (0,)), ((), ()))
    return lax.dot_general(left, right, contract, preferred_element_type=f32)


def cross_blocks(part):
    top = cross(part[:, :LANES], part)
    return jnp.stack([top[:, :LANES], top[:, LANES:], cross(part[:, LANES:], part[:, LANES:])])


def pack(low, mixed, high):
    row = lax.broadcasted_iota(jnp.int32, (LANES, LANES), 0)
    column = lax.broadcasted_iota(jnp.int32, (LANES, LANES), 1)
    shared = jnp.where(row <= column, low, high)
    diagonal = jnp.sum(jnp.where(row == column, high, 0.0), axis=0, keepdims=True)
    return mixed, shared, diagonal


def filter_kernel(
    snap_ref,
    prior_ref,
    coarse_ref,
    gram_ref,
    tile,
    prior_tile,
    ysum,
    edge,
    coarse,
    rounded,
    border,
    x_out,
    x_in,
    y_out,
    y_in,
    c_stage,
    c_out,
    c_in,
    blocks,
    packed,
    prior_gram,
    rs_in,
    z_in,
    ag_in,
    load_sem,
    store_sem,
    halo_send,
    halo_recv,
    rs_send,
    rs_recv,
    z_send,
    z_recv,
    ag_send,
    ag_recv,
):
    gx = lax.axis_index("gx")
    gy = lax.axis_index("gy")
    core = lax.rem(gy, 2)
    zed = gy // 2
    gx_next, gx_last = lax.rem(gx + 1, RING), lax.rem(gx + RING - 1, RING)
    gy_next, gy_last = lax.rem(gy + 1, RING), lax.rem(gy + RING - 1, RING)

    slabs = 16
    loads = []
    for m in range(PARTS):
        for q in range(FINE // slabs):
            place = (m, pl.ds(q * slabs, slabs))
            loads.append(
                pltpu.make_async_copy(
                    snap_ref.at[place], tile.at[place], load_sem.at[len(loads)]
                )
            )
    load_prior = pltpu.make_async_copy(prior_ref, prior_tile, load_sem.at[len(loads)])
    for load in loads:
        load.start()
    load_prior.start()

    barrier = pltpu.get_barrier_semaphore()

    def greet(peer):
        pl.semaphore_signal(barrier, inc=1, device_id=peer, device_id_type=MESH)

    def greet_z(step, carry):
        greet((gx, 2 * lax.rem(zed + step, DEEP) + core))
        return carry

    def greet_member(step, carry):
        other = lax.rem(gx * 2 + core + step, MEMBERS)
        greet((other // 2, 2 * zed + lax.rem(other, 2)))
        return carry

    lax.fori_loop(1, DEEP, greet_z, 0)
    lax.fori_loop(1, MEMBERS, greet_member, 0)
    for oy in (gy_last, gy_next):
        for ox in (gx_last, gx, gx_next):
            greet((ox, oy))
    for ox in (gx_last, gx_next):
        greet((ox, gy))

    halos = []

    def send(source, target, peer):
        copy = pltpu.make_async_remote_copy(
            src_ref=source,
            dst_ref=target,
            send_sem=halo_send.at[len(halos)],
            recv_sem=halo_recv.at[len(halos)],
            device_id=peer,
            device_id_type=MESH,
        )
        copy.start()
        halos.append(copy)

    c_stage[:, :, :, 8:, :] = jnp.zeros((2, 2, 2, 8, LANES), f32)
    taps = y_matrix()
    for m in range(PARTS):
        for q in range(FINE // slabs):
            loads[m * (FINE // slabs) + q].wait()
            for g in range(slabs // GROUP):
                first = q * slabs + g * GROUP
                fine = tile[m, pl.ds(first, GROUP)].reshape(GROUP * FINE, K)
                sums = jnp.dot(taps, fine, preferred_element_type=f32)
                ysum[m, pl.ds(first, GROUP)] = sums.reshape(GROUP, ROWS, K)

        for side in range(2):
            for step in range(2):
                cell = (-2, HALF)[side] + step
                value = x_sum(lambda x: ysum[m, x, pl.ds(0, HALF), :], cell)
                x_out[side, m, step] = value.astype(bf16)

        for slot in range(HALF + 4):
            value = x_sum(lambda x: ysum[m, x, pl.ds(HALF, 8), :], x_cell(slot))
            rows = pl.ds(m * (SLOTS * 8) + slot * 8, 8)
            edge[0, rows, :] = value[:, :LANES]
            edge[1, rows, :] = value[:, LANES:]
        for side in range(2):
            for step in range(2):
                start = m * SLOTS * 8 + side * 2 + step
                picked = [edge[h, pl.ds(start, HALF, stride=8), :] for h in range(2)]
                y_out[side, m, step] = jnp.concatenate(picked, axis=1).astype(bf16)
            for other in range(2):
                for along in range(2):
                    start = m * SLOTS * 8 + (HALF + other * 2 + along) * 8 + side * 2
                    for h in range(2):
                        c_stage[h, side, other, pl.ds((m * 2 + along) * 2, 2), :] = edge[
                            h, pl.ds(start, 2), :
                        ]

        if m >= 1:
            if m == 1:
                pl.semaphore_wait(barrier, DEEP - 1 + MEMBERS - 1 + 8)
            for part in (0, 1) if m == 1 else (m,):
                send(x_out.at[0, part], x_in.at[0, part], (gx_last, gy))
                send(x_out.at[1, part], x_in.at[1, part], (gx_next, gy))
                send(y_out.at[0, part], y_in.at[0, part], (gx, gy_last))
                send(y_out.at[1, part], y_in.at[1, part], (gx, gy_next))

    for side, oy in ((0, gy_last), (1, gy_next)):
        for other, ox in ((0, gx_last), (1, gx_next)):
            corner = [c_stage[h, side, other] for h in range(2)]
            c_out[side, other] = jnp.concatenate(corner, axis=1).astype(bf16)
            send(c_out.at[side, other], c_in.at[side, other], (ox, oy))

    along_y = lax.broadcasted_iota(jnp.int32, (16, LANES), 0)

    def inside(step, carry):
        m = step // 2
        row = pl.multiple_of(lax.rem(step, 2) * 16, 16)
        y = along_y + row
        kept = (y >= 2) & (y < HALF - 2)
        for h in range(2):
            lanes = pl.ds(h * LANES, LANES)
            for cell in range(HALF):
                value = x_sum(lambda x: ysum[m, x, pl.ds(row, 16), lanes], cell)
                rows = pl.ds(pl.multiple_of(m * (HALF * HALF) + cell * HALF + row, 16), 16)
                coarse[h, rows, :] = value
                rounded[rows, lanes] = jnp.where(kept, value, 0.0).astype(bf16)
        return carry

    lax.fori_loop(0, PARTS * 2, inside, 0)

    blocks[...] = jnp.zeros(blocks.shape, f32)
    size = (HALF - 4) * HALF // 2

    def cross_inside(step, carry):
        start = (step // 2) * HALF * HALF + 2 * HALF + lax.rem(step, 2) * size
        blocks[...] += cross_blocks(rounded[pl.ds(pl.multiple_of(start, 64), size), :])
        return carry

    lax.fori_loop(0, PARTS * 2, cross_inside, 0)

    load_prior.wait()
    squared = lax.dot_general(
        prior_tile[...],
        prior_tile[...],
        (((0,), (0,)), ((), ())),
        precision=lax.Precision.HIGHEST,
        preferred_element_type=f32,
    )
    mixed, shared, diagonal = pack(
        squared[:LANES, :LANES], squared[:LANES, LANES:], squared[LANES:, LANES:]
    )
    prior_gram[0:LANES, :] = mixed
    prior_gram[LANES:K, :] = shared
    prior_gram[K:, :] = jnp.broadcast_to(diagonal, (8, LANES))

    for copy in halos:
        copy.wait()
    for m in range(PARTS):
        for side in range(2):
            for step in range(2):
                cell = (HALF - 2, 0)[side] + step
                rows = pl.ds(m * HALF * HALF + cell * HALF, HALF)
                value = x_in[side, m, step].astype(f32)
                for h in range(2):
                    coarse[h, rows, :] += value[:, h * LANES : (h + 1) * LANES]
    for side in range(2):
        for other in range(2):
            corner = c_in[side, other].astype(f32)
            for m in range(PARTS):
                for along in range(2):
                    row = (HALF - 2, 0)[other] + along
                    column = (HALF - 2, 0)[side]
                    source = (m * 2 + along) * 2
                    target = pl.ds(m * HALF * HALF + row * HALF + column, 2)
                    value = corner[source : source + 2, :]
                    for h in range(2):
                        coarse[h, target, :] += value[:, h * LANES : (h + 1) * LANES]
    along_x = lax.broadcasted_iota(jnp.int32, (HALF, LANES), 0)
    kept = (along_x >= 2) & (along_x < HALF - 2)
    for m in range(PARTS):
        for side in range(2):
            for step in range(2):
                cell = (HALF - 2, 0)[side] + step
                rows = pl.ds(m * HALF * HALF + cell, HALF, stride=HALF)
                value = y_in[side, m, step].astype(f32)
                place = pl.ds(((m * 2 + side) * 2 + step) * HALF, HALF)
                for h in range(2):
                    total = coarse[h, rows, :] + value[:, h * LANES : (h + 1) * LANES]
                    coarse[h, rows, :] = total
                    border[place, pl.ds(h * LANES, LANES)] = jnp.where(kept, total, 0.0).astype(
                        bf16
                    )
    for m in range(PARTS):
        for side in range(2):
            rows = pl.ds(m * HALF * HALF + (HALF - 2, 0)[side] * HALF, 2 * HALF)
            place = pl.ds((PARTS * 4 + (m * 2 + side) * 2) * HALF, 2 * HALF)
            for h in range(2):
                border[place, pl.ds(h * LANES, LANES)] = coarse[h, rows, :].astype(bf16)

    total = blocks[...]
    half_border = PARTS * 4 * HALF
    for part in range(2):
        total += cross_blocks(border[pl.ds(part * half_border, half_border), :])
    mixed, shared, diagonal = pack(total[0], total[1], total[2])
    packed[0 : LANES // 8, 0:8, :] = mixed.reshape(LANES // 8, 8, LANES)
    packed[LANES // 8 :, 0:8, :] = shared.reshape(LANES // 8, 8, LANES)
    packed[:, 8:9, :] = jnp.broadcast_to(diagonal[None], (MEMBERS, 1, LANES))

    me = gx * 2 + core

    def to_members(source_of, target, send_sem, recv_sem):
        copies = []
        for step in range(1, MEMBERS):
            other = lax.rem(me + step, MEMBERS)
            copies.append(
                pltpu.make_async_remote_copy(
                    src_ref=source_of(other),
                    dst_ref=target.at[me],
                    send_sem=send_sem.at[step],
                    recv_sem=recv_sem.at[step],
                    device_id=(other // 2, 2 * zed + lax.rem(other, 2)),
                    device_id_type=MESH,
                )
            )
        for copy in copies:
            copy.start()
        return copies

    def sum_slots(slots, count):
        total = slots[0]
        for slot in range(1, count):
            total = total + slots[slot]
        return total

    copies = to_members(lambda other: packed.at[other], rs_in, rs_send, rs_recv)
    rs_in[me] = packed[me]

    block = 512

    def finish(step, carry):
        rows = pl.ds(pl.multiple_of(step * block, block), block)
        for h in range(2):
            rounded[rows, pl.ds(h * LANES, LANES)] = coarse[h, rows, :].astype(bf16)
        return carry

    lax.fori_loop(0, PARTS * HALF * HALF // block, finish, 0)
    store = pltpu.make_async_copy(rounded, coarse_ref, store_sem)
    store.start()
    for copy in copies:
        copy.wait()

    z_in[zed] = sum_slots(rs_in, MEMBERS)
    copies = []
    for step in range(1, DEEP):
        copies.append(
            pltpu.make_async_remote_copy(
                src_ref=z_in.at[zed],
                dst_ref=z_in.at[zed],
                send_sem=z_send.at[step],
                recv_sem=z_recv.at[step],
                device_id=(gx, 2 * lax.rem(zed + step, DEEP) + core),
                device_id_type=MESH,
            )
        )
    for copy in copies:
        copy.start()
    for copy in copies:
        copy.wait()

    ag_in[me] = sum_slots(z_in, DEEP)
    for copy in to_members(lambda other: ag_in.at[me], ag_in, ag_send, ag_recv):
        copy.wait()

    count = PARTS * HALF * HALF * RING * RING
    share = 1.0 / count
    sums = ag_in[:, 0:8, :].reshape(K, LANES)
    gram_ref[:K, :] = sums * share + prior_gram[:K, :]
    gram_ref[K:, :] = jnp.broadcast_to(ag_in[0, 8:9, :] * share, (8, LANES)) + prior_gram[K:, :]
    store.wait()


def filter_call(snapshots, prior):
    rows = PARTS * HALF * HALF
    vmem = pltpu.VMEM
    dma = pltpu.SemaphoreType.DMA
    return pl.pallas_call(
        filter_kernel,
        out_shape=(
            jax.ShapeDtypeStruct((rows, K), bf16),
            jax.ShapeDtypeStruct((K + 8, LANES), f32),
        ),
        in_specs=[pl.BlockSpec(memory_space=pltpu.HBM)] * 2,
        out_specs=(pl.BlockSpec(memory_space=pl.ANY), pl.BlockSpec(memory_space=pltpu.VMEM)),
        scratch_shapes=[
            vmem((PARTS, FINE, FINE, K), bf16),
            vmem((K, K), f32),
            vmem((PARTS, FINE, ROWS, K), f32),
            vmem((2, PARTS * SLOTS * 8, LANES), f32),
            vmem((2, rows, LANES), f32),
            vmem((rows, K), bf16),
            vmem((PARTS * 8 * HALF, K), bf16),
            vmem((2, PARTS, 2, HALF, K), bf16),
            vmem((2, PARTS, 2, HALF, K), bf16),
            vmem((2, PARTS, 2, HALF, K), bf16),
            vmem((2, PARTS, 2, HALF, K), bf16),
            vmem((2, 2, 2, 16, LANES), f32),
            vmem((2, 2, 16, K), bf16),
            vmem((2, 2, 16, K), bf16),
            vmem((3, LANES, LANES), f32),
            vmem((MEMBERS, 9, LANES), f32),
            vmem((K + 8, LANES), f32),
            vmem((MEMBERS, 9, LANES), f32),
            vmem((DEEP, 9, LANES), f32),
            vmem((MEMBERS, 9, LANES), f32),
            dma((13,)),
            dma,
            dma((16,)),
            dma((16,)),
            dma((MEMBERS,)),
            dma((MEMBERS,)),
            dma((DEEP,)),
            dma((DEEP,)),
            dma((MEMBERS,)),
            dma((MEMBERS,)),
        ],
        compiler_params=pltpu.CompilerParams(
            collective_id=0, has_side_effects=True, vmem_limit_bytes=48 * 2**20
        ),
        name="filter_and_gram",
    )(snapshots, prior)


def split(value):
    high = value.astype(bf16)
    rest = value - high.astype(f32)
    middle = rest.astype(bf16)
    return high, middle, (rest - middle.astype(f32)).astype(bf16)


def factor_panels(work, upper, inverse):
    below = lax.broadcasted_iota(jnp.int32, (PANEL, 128), 0)
    for first in range(0, K, PANEL):
        rows = pl.ds(first, PANEL)
        strip = work[rows, :]
        columns = [
            jnp.broadcast_to(strip[:, first + k : first + k + 1], (PANEL, 128))
            for k in range(PANEL)
        ]
        tiles = [strip[:, t : t + 128] for t in range(0, 2 * K, 128)]
        pivots = jnp.zeros((PANEL, 128), f32)
        for j in range(PANEL):
            pivot = jnp.broadcast_to(columns[j][j : j + 1, :], (PANEL, 128))
            pivots = jnp.where(below == j, pivot, pivots)
            if j == PANEL - 1:
                break
            factor = jnp.where(below > j, columns[j] / pivot, 0.0)
            for k in range(j + 1, PANEL):
                columns[k] -= factor * jnp.broadcast_to(columns[k][j : j + 1, :], (PANEL, 128))
            tiles = [t - factor * jnp.broadcast_to(t[j : j + 1, :], (PANEL, 128)) for t in tiles]
        scale = lax.rsqrt(pivots)
        strip = jnp.concatenate([t * scale for t in tiles], axis=1)
        upper[rows, :] = strip[:, :K]
        inverse[rows, :] = strip[:, K:]
        done = first + PANEL
        if done < K:
            high, middle, low = split(strip)
            left = jnp.concatenate([high, high, middle, high, low, middle], axis=0)
            right = jnp.concatenate([high, middle, high, low, high, middle], axis=0)
            work[done:, :] -= lax.dot_general(
                left[:, done:K], right, (((0,), (0,)), ((), ())), preferred_element_type=f32
            )


def factor_kernel(
    coarse_ref, gram_ref, modes_ref, upper_ref, rows_in, work, upper, inverse, out, load_sem, store_sem
):
    load = pltpu.make_async_copy(coarse_ref, rows_in, load_sem)
    load.start()
    row = lax.broadcasted_iota(jnp.int32, (K, K), 0)
    column = lax.broadcasted_iota(jnp.int32, (K, K), 1)
    shared = gram_ref[LANES:K, :]
    turned = shared.T
    upper_half = row[:LANES, :LANES] <= column[:LANES, :LANES]
    equal = row[:LANES, :LANES] == column[:LANES, :LANES]
    work[:LANES, :LANES] = jnp.where(upper_half, shared, turned)
    work[:LANES, LANES:K] = gram_ref[:LANES, :]
    work[LANES:, :LANES] = jnp.zeros((LANES, LANES), f32)
    work[LANES:, LANES:K] = jnp.where(
        equal, gram_ref[K : K + 1, :], jnp.where(upper_half, turned, shared)
    )
    work[:, K:] = jnp.where(row == column, 1.0, 0.0)
    factor_panels(work, upper, inverse)
    upper_ref[...] = jnp.where(row <= column, upper[...], 0.0)
    high, middle, low = split(inverse[...].T)
    load.wait()
    count = rows_in.shape[0]
    block = 512
    stores = []
    for step in range(count // block):
        rows = pl.ds(step * block, block)
        part = rows_in[rows, :]
        value = jnp.dot(part, high, preferred_element_type=f32)
        value += jnp.dot(part, middle, preferred_element_type=f32)
        out[rows, :] = value
        stores.append(
            pltpu.make_async_copy(out.at[rows], modes_ref.at[rows], store_sem.at[step])
        )
        stores[-1].start()
    for store in stores:
        store.wait()


def factor_call(coarse, gram):
    rows = coarse.shape[0]
    vmem = pltpu.VMEM
    return pl.pallas_call(
        factor_kernel,
        out_shape=(jax.ShapeDtypeStruct((rows, K), f32), jax.ShapeDtypeStruct((K, K), f32)),
        in_specs=[pl.BlockSpec(memory_space=pl.ANY), pl.BlockSpec(memory_space=pltpu.VMEM)],
        out_specs=(pl.BlockSpec(memory_space=pl.ANY), pl.BlockSpec(memory_space=pltpu.VMEM)),
        scratch_shapes=[
            vmem((rows, K), bf16),
            vmem((K, 2 * K), f32),
            vmem((K, K), f32),
            vmem((K, K), f32),
            vmem((rows, K), f32),
            pltpu.SemaphoreType.DMA,
            pltpu.SemaphoreType.DMA((rows // 512,)),
        ],
        compiler_params=pltpu.CompilerParams(vmem_limit_bytes=48 * 2**20),
        name="factor_and_modes",
    )(coarse, gram)


def shards(snapshots, prior):
    coarse, gram = filter_call(snapshots, prior)
    modes, upper = factor_call(coarse, gram)
    return (modes.reshape(PARTS, HALF, HALF, K), upper)


def solution(mesh):
    return jax.shard_map(
        shards,
        mesh=mesh,
        in_specs=(P(None, "gx", "gy", None), P()),
        out_specs=(P(None, "gx", "gy", None), P()),
        check_vma=False,
    )
```

time: 50.9 us -> 48.4 us (0.951)
  Pallas kernels: 49.1 us -> 46.7 us
    pallas_call x1, Pallas kernels: 38 us -> 35.5 us  [filter_call(): pl.pallas_call(filter_kernel, out_shape=(jax.ShapeDtypeStruct((rows, K),...]
where the time goes in v2:
time: 48.4 us; the launch traced here: 48.2 us
  Pallas kernels  46.7 us (96%)
  local copies, waits for them, and re-layouts  0.94 us (2%)
  between operations  0.65 us (1%)
    pallas_call x1, Pallas kernels, filter_call(): pl.pallas_call(filter_kernel, out_shape=(jax.ShapeDtypeStruct((rows, K),...  35.5 us
    pallas_call x1, Pallas kernels, factor_call(): pl.pallas_call(factor_kernel, out_shape=(jax.ShapeDtypeStruct((rows, K),...  11.1 us

profile of v2, /device:TPU:1, one launch (start us, length us, event | category | flops | bytes accessed | tf_op | source)
XLA Modules:
  0.0 48.2 jit_solution(10715665231450284523)
XLA Ops:
  0.6 0.0 copy-start
  0.6 0.9 %copy-done = f32[256,256]{1,0:T(8,128)S(1)} copy-done((f32[256,256]{1,0:T(8,128)S(1)}, f32[256,256]{1,0:T(8,128)}, u32[]{:S(2)}) %copy-start) | copy-done | bytes 262168
  1.6 35.5 %filter_and_gram.1 = (bf16[3072,256]{1,0:T(8,128)(2,1)S(1)}, f32[264,128]{1,0:T(8,128)S(1)}) custom-call(bf16[3,64,64,256]{3,2,1,0:T(8,128)(2,1)} %snap_ref.1, f32[256,256]{1,0:T(8,128)S(1)} %copy-done), custom_call_target="tpu_custom_call" | custom-call | tf_op jit(solution)/shard_map/filter_and_gram/pallas_call | solution.py:403
  37.1 11.1 %factor_and_modes.1 = (f32[3072,256]{1,0:T(8,128)}, f32[256,256]{1,0:T(8,128)}) custom-call(bf16[3072,256]{1,0:T(8,128)(2,1)S(1)} %get-tuple-element.6.coarse_ref, f32[264,128]{1,0:T(8,128)S(1)} %get-tuple-element.7.gram_ref), custom_call_target="tpu_custom_call" | custom-call | tf_op jit(solution)/shard_map/factor_and_modes/pallas_call | solution.py:533
Async XLA Ops:
  0.6 1.0 %copy-start = (f32[256,256]{1,0:T(8,128)S(1)}, f32[256,256]{1,0:T(8,128)}, u32[]{:S(2)}) copy-start(f32[256,256]{1,0:T(8,128)} %prior_ref.1) | copy-start | bytes 786436

commit v3 on v2

--- a/solution.py
+++ b/solution.py
@@ -1,3 +1,5 @@
+import functools
+
 import jax
 import jax.numpy as jnp
 from jax import lax
@@ -18,9 +20,10 @@
 ROWS = 40
 GROUP = 4
 SLOTS = 40
+SIDE = 4
 DEEP = 8
 MEMBERS = 32
-PANEL = 16
+PANEL = 32
 
 
 def y_matrix():
@@ -83,13 +86,15 @@
     return mixed, shared, diagonal
 
 
+def arrivals(ref, sem):
+    pltpu.make_async_copy(ref, ref, sem).wait()
+
+
 def filter_kernel(
     snap_ref,
-    prior_ref,
     coarse_ref,
     gram_ref,
     tile,
-    prior_tile,
     ysum,
     edge,
     coarse,
@@ -104,7 +109,6 @@
     c_in,
     blocks,
     packed,
-    prior_gram,
     rs_in,
     z_in,
     ag_in,
@@ -112,12 +116,8 @@
     store_sem,
     halo_send,
     halo_recv,
-    rs_send,
-    rs_recv,
-    z_send,
-    z_recv,
-    ag_send,
-    ag_recv,
+    sum_send,
+    sum_recv,
 ):
     gx = lax.axis_index("gx")
     gy = lax.axis_index("gy")
@@ -126,7 +126,7 @@
     gx_next, gx_last = lax.rem(gx + 1, RING), lax.rem(gx + RING - 1, RING)
     gy_next, gy_last = lax.rem(gy + 1, RING), lax.rem(gy + RING - 1, RING)
 
-    slabs = 16
+    slabs = 32
     loads = []
     for m in range(PARTS):
         for q in range(FINE // slabs):
@@ -136,10 +136,8 @@
                     snap_ref.at[place], tile.at[place], load_sem.at[len(loads)]
                 )
             )
-    load_prior = pltpu.make_async_copy(prior_ref, prior_tile, load_sem.at[len(loads)])
     for load in loads:
         load.start()
-    load_prior.start()
 
     barrier = pltpu.get_barrier_semaphore()
 
@@ -163,19 +161,15 @@
     for ox in (gx_last, gx_next):
         greet((ox, gy))
 
-    halos = []
-
-    def send(source, target, peer):
-        copy = pltpu.make_async_remote_copy(
+    def send(source, target, peer, kind):
+        pltpu.make_async_remote_copy(
             src_ref=source,
             dst_ref=target,
-            send_sem=halo_send.at[len(halos)],
-            recv_sem=halo_recv.at[len(halos)],
+            send_sem=halo_send.at[kind],
+            recv_sem=halo_recv.at[kind],
             device_id=peer,
             device_id_type=MESH,
-        )
-        copy.start()
-        halos.append(copy)
+        ).start()
 
     c_stage[:, :, :, 8:, :] = jnp.zeros((2, 2, 2, 8, LANES), f32)
     taps = y_matrix()
@@ -216,16 +210,16 @@
             if m == 1:
                 pl.semaphore_wait(barrier, DEEP - 1 + MEMBERS - 1 + 8)
             for part in (0, 1) if m == 1 else (m,):
-                send(x_out.at[0, part], x_in.at[0, part], (gx_last, gy))
-                send(x_out.at[1, part], x_in.at[1, part], (gx_next, gy))
-                send(y_out.at[0, part], y_in.at[0, part], (gx, gy_last))
-                send(y_out.at[1, part], y_in.at[1, part], (gx, gy_next))
+                send(x_out.at[0, part], x_in.at[0, part], (gx_last, gy), 0)
+                send(x_out.at[1, part], x_in.at[1, part], (gx_next, gy), 0)
+                send(y_out.at[0, part], y_in.at[0, part], (gx, gy_last), 1)
+                send(y_out.at[1, part], y_in.at[1, part], (gx, gy_next), 1)
 
     for side, oy in ((0, gy_last), (1, gy_next)):
         for other, ox in ((0, gx_last), (1, gx_next)):
             corner = [c_stage[h, side, other] for h in range(2)]
             c_out[side, other] = jnp.concatenate(corner, axis=1).astype(bf16)
-            send(c_out.at[side, other], c_in.at[side, other], (ox, oy))
+            send(c_out.at[side, other], c_in.at[side, other], (ox, oy), 2)
 
     along_y = lax.broadcasted_iota(jnp.int32, (16, LANES), 0)
 
@@ -255,23 +249,8 @@
 
     lax.fori_loop(0, PARTS * 2, cross_inside, 0)
 
-    load_prior.wait()
-    squared = lax.dot_general(
-        prior_tile[...],
-        prior_tile[...],
-        (((0,), (0,)), ((), ())),
-        precision=lax.Precision.HIGHEST,
-        preferred_element_type=f32,
-    )
-    mixed, shared, diagonal = pack(
-        squared[:LANES, :LANES], squared[:LANES, LANES:], squared[LANES:, LANES:]
-    )
-    prior_gram[0:LANES, :] = mixed
-    prior_gram[LANES:K, :] = shared
-    prior_gram[K:, :] = jnp.broadcast_to(diagonal, (8, LANES))
-
-    for copy in halos:
-        copy.wait()
+    for kind, arrived in enumerate((x_in, y_in, c_in)):
+        arrivals(arrived, halo_recv.at[kind])
     for m in range(PARTS):
         for side in range(2):
             for step in range(2):
@@ -325,23 +304,27 @@
 
     me = gx * 2 + core
 
-    def to_members(source_of, target, send_sem, recv_sem):
-        copies = []
-        for step in range(1, MEMBERS):
-            other = lax.rem(me + step, MEMBERS)
-            copies.append(
-                pltpu.make_async_remote_copy(
-                    src_ref=source_of(other),
-                    dst_ref=target.at[me],
-                    send_sem=send_sem.at[step],
-                    recv_sem=recv_sem.at[step],
-                    device_id=(other // 2, 2 * zed + lax.rem(other, 2)),
-                    device_id_type=MESH,
-                )
-            )
-        for copy in copies:
-            copy.start()
-        return copies
+    at_x, at_y = gx // SIDE, lax.rem(gx, SIDE)
+
+    def to_members(source_of, target, phase):
+        for far in range(SIDE, -1, -1):
+            for dx in range(SIDE):
+                for dy in range(SIDE):
+                    if min(dx, SIDE - dx) + min(dy, SIDE - dy) != far:
+                        continue
+                    peer = SIDE * lax.rem(at_x + dx, SIDE) + lax.rem(at_y + dy, SIDE)
+                    for dc in range(2):
+                        if dx + dy + dc == 0:
+                            continue
+                        there = lax.rem(core + dc, 2)
+                        pltpu.make_async_remote_copy(
+                            src_ref=source_of(peer * 2 + there),
+                            dst_ref=target.at[me],
+                            send_sem=sum_send.at[phase],
+                            recv_sem=sum_recv.at[phase],
+                            device_id=(peer, 2 * zed + there),
+                            device_id_type=MESH,
+                        ).start()
 
     def sum_slots(slots, count):
         total = slots[0]
@@ -349,7 +332,7 @@
             total = total + slots[slot]
         return total
 
-    copies = to_members(lambda other: packed.at[other], rs_in, rs_send, rs_recv)
+    to_members(lambda other: packed.at[other], rs_in, 0)
     rs_in[me] = packed[me]
 
     block = 512
@@ -363,40 +346,37 @@
     lax.fori_loop(0, PARTS * HALF * HALF // block, finish, 0)
     store = pltpu.make_async_copy(rounded, coarse_ref, store_sem)
     store.start()
-    for copy in copies:
-        copy.wait()
+    arrivals(rs_in.at[pl.ds(0, MEMBERS - 1)], sum_recv.at[0])
 
     z_in[zed] = sum_slots(rs_in, MEMBERS)
-    copies = []
-    for step in range(1, DEEP):
-        copies.append(
-            pltpu.make_async_remote_copy(
-                src_ref=z_in.at[zed],
-                dst_ref=z_in.at[zed],
-                send_sem=z_send.at[step],
-                recv_sem=z_recv.at[step],
-                device_id=(gx, 2 * lax.rem(zed + step, DEEP) + core),
-                device_id_type=MESH,
-            )
-        )
-    for copy in copies:
-        copy.start()
-    for copy in copies:
-        copy.wait()
+    for step in (4, 3, 5, 2, 6, 1, 7):
+        pltpu.make_async_remote_copy(
+            src_ref=z_in.at[zed],
+            dst_ref=z_in.at[zed],
+            send_sem=sum_send.at[1],
+            recv_sem=sum_recv.at[1],
+            device_id=(gx, 2 * lax.rem(zed + step, DEEP) + core),
+            device_id_type=MESH,
+        ).start()
+    arrivals(z_in.at[pl.ds(0, DEEP - 1)], sum_recv.at[1])
 
     ag_in[me] = sum_slots(z_in, DEEP)
-    for copy in to_members(lambda other: ag_in.at[me], ag_in, ag_send, ag_recv):
-        copy.wait()
+    to_members(lambda other: ag_in.at[me], ag_in, 2)
+    arrivals(ag_in.at[pl.ds(0, MEMBERS - 1)], sum_recv.at[2])
 
     count = PARTS * HALF * HALF * RING * RING
     share = 1.0 / count
-    sums = ag_in[:, 0:8, :].reshape(K, LANES)
-    gram_ref[:K, :] = sums * share + prior_gram[:K, :]
-    gram_ref[K:, :] = jnp.broadcast_to(ag_in[0, 8:9, :] * share, (8, LANES)) + prior_gram[K:, :]
+    gram_ref[:K, :] = ag_in[:, 0:8, :].reshape(K, LANES) * share
+    gram_ref[K:, :] = jnp.broadcast_to(ag_in[0, 8:9, :] * share, (8, LANES))
+    for kind, sent in enumerate((x_out, y_out, c_out)):
+        arrivals(sent, halo_send.at[kind])
+    arrivals(packed.at[pl.ds(0, MEMBERS - 1)], sum_send.at[0])
+    arrivals(z_in.at[pl.ds(0, DEEP - 1)], sum_send.at[1])
+    arrivals(ag_in.at[pl.ds(0, MEMBERS - 1)], sum_send.at[2])
     store.wait()
 
 
-def filter_call(snapshots, prior):
+def filter_call(snapshots):
     rows = PARTS * HALF * HALF
     vmem = pltpu.VMEM
     dma = pltpu.SemaphoreType.DMA
@@ -406,11 +386,10 @@
             jax.ShapeDtypeStruct((rows, K), bf16),
             jax.ShapeDtypeStruct((K + 8, LANES), f32),
         ),
-        in_specs=[pl.BlockSpec(memory_space=pltpu.HBM)] * 2,
+        in_specs=[pl.BlockSpec(memory_space=pltpu.HBM)],
         out_specs=(pl.BlockSpec(memory_space=pl.ANY), pl.BlockSpec(memory_space=pltpu.VMEM)),
         scratch_shapes=[
             vmem((PARTS, FINE, FINE, K), bf16),
-            vmem((K, K), f32),
             vmem((PARTS, FINE, ROWS, K), f32),
             vmem((2, PARTS * SLOTS * 8, LANES), f32),
             vmem((2, rows, LANES), f32),
@@ -425,26 +404,21 @@
             vmem((2, 2, 16, K), bf16),
             vmem((3, LANES, LANES), f32),
             vmem((MEMBERS, 9, LANES), f32),
-            vmem((K + 8, LANES), f32),
             vmem((MEMBERS, 9, LANES), f32),
             vmem((DEEP, 9, LANES), f32),
             vmem((MEMBERS, 9, LANES), f32),
-            dma((13,)),
+            dma((PARTS * 2,)),
             dma,
-            dma((16,)),
-            dma((16,)),
-            dma((MEMBERS,)),
-            dma((MEMBERS,)),
-            dma((DEEP,)),
-            dma((DEEP,)),
-            dma((MEMBERS,)),
-            dma((MEMBERS,)),
+            dma((3,)),
+            dma((3,)),
+            dma((3,)),
+            dma((3,)),
         ],
         compiler_params=pltpu.CompilerParams(
             collective_id=0, has_side_effects=True, vmem_limit_bytes=48 * 2**20
         ),
         name="filter_and_gram",
-    )(snapshots, prior)
+    )(snapshots)
 
 
 def split(value):
@@ -455,55 +429,114 @@
 
 
 def factor_panels(work, upper, inverse):
-    below = lax.broadcasted_iota(jnp.int32, (PANEL, 128), 0)
+    place = lax.broadcasted_iota(jnp.int32, (8, LANES), 0)
+    parts = PANEL // 8
+    contract = (((0,), (0,)), ((), ()))
+
+    def spread(value, row):
+        return jnp.broadcast_to(value[row : row + 1, :], (8, LANES))
+
+    later = None
     for first in range(0, K, PANEL):
         rows = pl.ds(first, PANEL)
-        strip = work[rows, :]
+        low = 0 if first < LANES else LANES
+        high = low + 3 * LANES
+        strip = work[rows, low:high]
         columns = [
-            jnp.broadcast_to(strip[:, first + k : first + k + 1], (PANEL, 128))
+            [
+                jnp.broadcast_to(
+                    strip[8 * t : 8 * t + 8, first - low + k : first - low + k + 1], (8, LANES)
+                )
+                if t >= k // 8
+                else None
+                for t in range(parts)
+            ]
             for k in range(PANEL)
         ]
-        tiles = [strip[:, t : t + 128] for t in range(0, 2 * K, 128)]
-        pivots = jnp.zeros((PANEL, 128), f32)
+        tiles = [
+            [strip[8 * t : 8 * t + 8, q * LANES : (q + 1) * LANES] for q in range(3)]
+            for t in range(parts)
+        ]
+        pivots = [None] * parts
+        pivot = spread(columns[0][0], 0)
         for j in range(PANEL):
-            pivot = jnp.broadcast_to(columns[j][j : j + 1, :], (PANEL, 128))
-            pivots = jnp.where(below == j, pivot, pivots)
+            top, row = divmod(j, 8)
+            column = columns[j]
+            pivots[top] = pivot if row == 0 else jnp.where(place == row, pivot, pivots[top])
             if j == PANEL - 1:
                 break
-            factor = jnp.where(below > j, columns[j] / pivot, 0.0)
+            if j == 2 and later is not None:
+                later()
+                later = None
+            over = 1.0 / pivot
+            beside = spread(column[(j + 1) // 8], (j + 1) % 8)
+            pivot = spread(columns[j + 1][(j + 1) // 8], (j + 1) % 8) - (beside * beside) * over
+            factor = {}
+            for t in range(top if row < 7 else top + 1, parts):
+                value = column[t] * over
+                factor[t] = jnp.where(place > row, value, 0.0) if t == top else value
             for k in range(j + 1, PANEL):
-                columns[k] -= factor * jnp.broadcast_to(columns[k][j : j + 1, :], (PANEL, 128))
-            tiles = [t - factor * jnp.broadcast_to(t[j : j + 1, :], (PANEL, 128)) for t in tiles]
-        scale = lax.rsqrt(pivots)
-        strip = jnp.concatenate([t * scale for t in tiles], axis=1)
-        upper[rows, :] = strip[:, :K]
-        inverse[rows, :] = strip[:, K:]
+                across = spread(column[k // 8], k % 8)
+                for t in range(k // 8, parts):
+                    columns[k][t] = columns[k][t] - factor[t] * across
+            source = [spread(value, row) for value in tiles[top]]
+            for t in factor:
+                tiles[t] = [tiles[t][q] - factor[t] * source[q] for q in range(3)]
+        strip = jnp.concatenate(
+            [
+                jnp.concatenate([value * lax.rsqrt(pivots[t]) for value in tiles[t]], axis=1)
+                for t in range(parts)
+            ],
+            axis=0,
+        )
+        if low == 0:
+            upper[rows, :] = strip[:, :K]
+            inverse[rows, :LANES] = strip[:, K:]
+            inverse[rows, LANES:] = jnp.zeros((PANEL, LANES), f32)
+        else:
+            upper[rows, :LANES] = jnp.zeros((PANEL, LANES), f32)
+            upper[rows, LANES:] = strip[:, :LANES]
+            inverse[rows, :] = strip[:, LANES:]
         done = first + PANEL
         if done < K:
-            high, middle, low = split(strip)
-            left = jnp.concatenate([high, high, middle, high, low, middle], axis=0)
-            right = jnp.concatenate([high, middle, high, low, high, middle], axis=0)
-            work[done:, :] -= lax.dot_general(
-                left[:, done:K], right, (((0,), (0,)), ((), ())), preferred_element_type=f32
-            )
+            great, middle, small = split(strip)
+            left = jnp.concatenate([great, great, middle, great, small, middle], axis=0)
+            right = jnp.concatenate([great, middle, great, small, great, middle], axis=0)
+
+            def update(start, stop, left=left, right=right, low=low, high=high):
+                work[start:stop, low:high] -= lax.dot_general(
+                    left[:, start - low : stop - low], right, contract, preferred_element_type=f32
+                )
+
+            update(done, done + PANEL)
+            if done + PANEL < K:
+                later = functools.partial(update, done + PANEL, K)
 
 
 def factor_kernel(
-    coarse_ref, gram_ref, modes_ref, upper_ref, rows_in, work, upper, inverse, out, load_sem, store_sem
+    coarse_ref, gram_ref, prior_ref, modes_ref, upper_ref, rows_in, work, upper, inverse, out, load_sem, store_sem
 ):
     load = pltpu.make_async_copy(coarse_ref, rows_in, load_sem)
     load.start()
     row = lax.broadcasted_iota(jnp.int32, (K, K), 0)
     column = lax.broadcasted_iota(jnp.int32, (K, K), 1)
+    prior_gram = lax.dot_general(
+        prior_ref[...],
+        prior_ref[...],
+        (((0,), (0,)), ((), ())),
+        precision=lax.Precision.HIGHEST,
+        preferred_element_type=f32,
+    )
     shared = gram_ref[LANES:K, :]
     turned = shared.T
     upper_half = row[:LANES, :LANES] <= column[:LANES, :LANES]
     equal = row[:LANES, :LANES] == column[:LANES, :LANES]
-    work[:LANES, :LANES] = jnp.where(upper_half, shared, turned)
-    work[:LANES, LANES:K] = gram_ref[:LANES, :]
+    work[:LANES, :LANES] = jnp.where(upper_half, shared, turned) + prior_gram[:LANES, :LANES]
+    work[:LANES, LANES:K] = gram_ref[:LANES, :] + prior_gram[:LANES, LANES:]
     work[LANES:, :LANES] = jnp.zeros((LANES, LANES), f32)
-    work[LANES:, LANES:K] = jnp.where(
-        equal, gram_ref[K : K + 1, :], jnp.where(upper_half, turned, shared)
+    work[LANES:, LANES:K] = (
+        jnp.where(equal, gram_ref[K : K + 1, :], jnp.where(upper_half, turned, shared))
+        + prior_gram[LANES:, LANES:]
     )
     work[:, K:] = jnp.where(row == column, 1.0, 0.0)
     factor_panels(work, upper, inverse)
@@ -512,28 +545,23 @@
     load.wait()
     count = rows_in.shape[0]
     block = 512
-    stores = []
     for step in range(count // block):
         rows = pl.ds(step * block, block)
         part = rows_in[rows, :]
         value = jnp.dot(part, high, preferred_element_type=f32)
         value += jnp.dot(part, middle, preferred_element_type=f32)
         out[rows, :] = value
-        stores.append(
-            pltpu.make_async_copy(out.at[rows], modes_ref.at[rows], store_sem.at[step])
-        )
-        stores[-1].start()
-    for store in stores:
-        store.wait()
-
-
-def factor_call(coarse, gram):
+        pltpu.make_async_copy(out.at[rows], modes_ref.at[rows], store_sem).start()
+    pltpu.make_async_copy(out, modes_ref, store_sem).wait()
+
+
+def factor_call(coarse, gram, prior):
     rows = coarse.shape[0]
     vmem = pltpu.VMEM
     return pl.pallas_call(
         factor_kernel,
         out_shape=(jax.ShapeDtypeStruct((rows, K), f32), jax.ShapeDtypeStruct((K, K), f32)),
-        in_specs=[pl.BlockSpec(memory_space=pl.ANY), pl.BlockSpec(memory_space=pltpu.VMEM)],
+        in_specs=[pl.BlockSpec(memory_space=pl.ANY)] + [pl.BlockSpec(memory_space=pltpu.VMEM)] * 2,
         out_specs=(pl.BlockSpec(memory_space=pl.ANY), pl.BlockSpec(memory_space=pltpu.VMEM)),
         scratch_shapes=[
             vmem((rows, K), bf16),
@@ -542,16 +570,16 @@
             vmem((K, K), f32),
             vmem((rows, K), f32),
             pltpu.SemaphoreType.DMA,
-            pltpu.SemaphoreType.DMA((rows // 512,)),
+            pltpu.SemaphoreType.DMA,
         ],
         compiler_params=pltpu.CompilerParams(vmem_limit_bytes=48 * 2**20),
         name="factor_and_modes",
-    )(coarse, gram)
+    )(coarse, gram, prior)
 
 
 def shards(snapshots, prior):
-    coarse, gram = filter_call(snapshots, prior)
-    modes, upper = factor_call(coarse, gram)
+    coarse, gram = filter_call(snapshots)
+    modes, upper = factor_call(coarse, gram, prior)
     return (modes.reshape(PARTS, HALF, HALF, K), upper)
 
 

time: 48.4 us -> 43.9 us (0.907)
  Pallas kernels: 46.7 us -> 43.2 us
  local copies, waits for them, and re-layouts: 0.94 us -> 0.01 us
    pallas_call x1, Pallas kernels: 35.5 us -> 33.1 us  [filter_call(): pl.pallas_call(filter_kernel, out_shape=(jax.ShapeDtypeStruct((rows, K),...]
    pallas_call x1, Pallas kernels: 11.1 us -> 10.1 us  [factor_call(): pl.pallas_call(factor_kernel, out_shape=(jax.ShapeDtypeStruct((rows, K),...]
    unnamed x2, local copies, waits for them, and re-layouts: 0.94 us -> 0.01 us
where the time goes in v3:
time: 43.9 us; the launch traced here: 43.8 us
  Pallas kernels  43.2 us (98%)
  between operations  0.65 us (1%)
    pallas_call x1, Pallas kernels, filter_call(): pl.pallas_call(filter_kernel, out_shape=(jax.ShapeDtypeStruct((rows, K),...  33.1 us
    pallas_call x1, Pallas kernels, factor_call(): pl.pallas_call(factor_kernel, out_shape=(jax.ShapeDtypeStruct((rows, K),...  10.1 us

profile of v3, /device:TPU:1, one launch (start us, length us, event | category | flops | bytes accessed | tf_op | source)
XLA Modules:
  0.0 43.8 jit_solution(1747360742272033673)
XLA Ops:
  0.6 0.0 copy-start
  0.6 33.1 %filter_and_gram.1 = (bf16[3072,256]{1,0:T(8,128)(2,1)S(1)}, f32[264,128]{1,0:T(8,128)S(1)}) custom-call(bf16[3,64,64,256]{3,2,1,0:T(8,128)(2,1)} %snap_ref.1), custom_call_target="tpu_custom_call" | custom-call | tf_op jit(solution)/shard_map/filter_and_gram/pallas_call | solution.py:383
  33.7 0.0 copy-done
  33.7 10.1 %factor_and_modes.1 = (f32[3072,256]{1,0:T(8,128)}, f32[256,256]{1,0:T(8,128)}) custom-call(bf16[3072,256]{1,0:T(8,128)(2,1)S(1)} %get-tuple-element.6.coarse_ref, f32[264,128]{1,0:T(8,128)S(1)} %get-tuple-element.7.gram_ref, f32[256,256]{1,0:T(8,128)S(1)} %copy-done), custom_call_target="tpu_custom_call" | custom-call | tf_op jit(solution)/shard_map/factor_and_modes/pallas_call | solution.py:561
Async XLA Ops:
  0.6 33.1 %copy-start = (f32[256,256]{1,0:T(8,128)S(1)}, f32[256,256]{1,0:T(8,128)}, u32[]{:S(2)}) copy-start(f32[256,256]{1,0:T(8,128)} %prior_ref.1) | copy-start | bytes 786436

commit v4 on v3

--- a/solution.py
+++ b/solution.py
@@ -17,7 +17,7 @@
 HALF = 32
 K = 256
 LANES = 128
-ROWS = 40
+STRIP = 16
 GROUP = 4
 SLOTS = 40
 SIDE = 4
@@ -26,19 +26,30 @@
 PANEL = 32
 
 
-def y_matrix():
-    shape = (GROUP * ROWS, GROUP * FINE)
+def tap_matrix(row_slab, cell, column_slab, y, used):
+    offset = jnp.where((row_slab == column_slab) & used, y - 2 * cell + 4, -1)
+    taps = jnp.zeros(offset.shape, f32)
+    for place, tap in enumerate(TAPS):
+        taps = jnp.where(offset == place, tap / 65536.0, taps)
+    return jnp.where(row_slab % 2 == 1, 8.0 * taps, taps).astype(bf16)
+
+
+def inside_taps():
+    shape = (GROUP * HALF, GROUP * FINE)
     row = lax.broadcasted_iota(jnp.int32, shape, 0)
     column = lax.broadcasted_iota(jnp.int32, shape, 1)
-    slab = row // ROWS
-    index = row % ROWS
-    cell = jnp.where(index < HALF, index, jnp.where(index < HALF + 2, index - HALF - 2, index - 2))
-    offset = column % FINE - 2 * cell + 4
-    offset = jnp.where((slab == column // FINE) & (index < HALF + 4), offset, -1)
-    taps = jnp.zeros(shape, f32)
-    for place, tap in enumerate(TAPS):
-        taps = jnp.where(offset == place, tap / 65536.0, taps)
-    return jnp.where(slab % 2 == 1, 8.0 * taps, taps).astype(bf16)
+    return tap_matrix(row // HALF, row % HALF, column // FINE, column % FINE, row >= 0)
+
+
+def outside_taps():
+    shape = (8 * 8, 8 * 2 * STRIP)
+    row = lax.broadcasted_iota(jnp.int32, shape, 0)
+    column = lax.broadcasted_iota(jnp.int32, shape, 1)
+    index = row % 8
+    cell = jnp.where(index < 2, index - 2, index + HALF - 2)
+    along = column % (2 * STRIP)
+    y = jnp.where(along < STRIP, along, along + FINE - 2 * STRIP)
+    return tap_matrix(row // 8, cell, column // (2 * STRIP), y, index < 4)
 
 
 def x_sum(load, cell):
@@ -95,7 +106,9 @@
     coarse_ref,
     gram_ref,
     tile,
+    strip,
     ysum,
+    yside,
     edge,
     coarse,
     rounded,
@@ -126,14 +139,23 @@
     gx_next, gx_last = lax.rem(gx + 1, RING), lax.rem(gx + RING - 1, RING)
     gy_next, gy_last = lax.rem(gy + 1, RING), lax.rem(gy + RING - 1, RING)
 
-    slabs = 32
+    for first in (0, FINE - GROUP):
+        place = (slice(None), pl.ds(first, GROUP))
+        pltpu.make_async_copy(snap_ref.at[place], tile.at[place], load_sem.at[0]).start()
+    for side in range(2):
+        pltpu.make_async_copy(
+            snap_ref.at[:, :, pl.ds(side * (FINE - STRIP), STRIP)],
+            strip.at[:, :, pl.ds(side * STRIP, STRIP)],
+            load_sem.at[1],
+        ).start()
+    slabs = (FINE - 2 * GROUP) // 2
     loads = []
     for m in range(PARTS):
-        for q in range(FINE // slabs):
-            place = (m, pl.ds(q * slabs, slabs))
+        for q in range(2):
+            place = (m, pl.ds(GROUP + q * slabs, slabs))
             loads.append(
                 pltpu.make_async_copy(
-                    snap_ref.at[place], tile.at[place], load_sem.at[len(loads)]
+                    snap_ref.at[place], tile.at[place], load_sem.at[2 + len(loads)]
                 )
             )
     for load in loads:
@@ -172,24 +194,32 @@
         ).start()
 
     c_stage[:, :, :, 8:, :] = jnp.zeros((2, 2, 2, 8, LANES), f32)
-    taps = y_matrix()
+    taps = inside_taps()
+
+    def y_pass(m, first):
+        fine = tile[m, pl.ds(first, GROUP)].reshape(GROUP * FINE, K)
+        sums = jnp.dot(taps, fine, preferred_element_type=f32)
+        ysum[m, pl.ds(first, GROUP)] = sums.reshape(GROUP, HALF, K)
+
+    arrivals(tile.at[:, pl.ds(0, 2 * GROUP)], load_sem.at[0])
     for m in range(PARTS):
-        for q in range(FINE // slabs):
-            loads[m * (FINE // slabs) + q].wait()
-            for g in range(slabs // GROUP):
-                first = q * slabs + g * GROUP
-                fine = tile[m, pl.ds(first, GROUP)].reshape(GROUP * FINE, K)
-                sums = jnp.dot(taps, fine, preferred_element_type=f32)
-                ysum[m, pl.ds(first, GROUP)] = sums.reshape(GROUP, ROWS, K)
-
+        y_pass(m, 0)
+        y_pass(m, FINE - GROUP)
         for side in range(2):
             for step in range(2):
                 cell = (-2, HALF)[side] + step
-                value = x_sum(lambda x: ysum[m, x, pl.ds(0, HALF), :], cell)
+                value = x_sum(lambda x: ysum[m, x], cell)
                 x_out[side, m, step] = value.astype(bf16)
 
+    outer = outside_taps()
+    arrivals(strip, load_sem.at[1])
+    for m in range(PARTS):
+        for g in range(FINE // 8):
+            fine = strip[m, pl.ds(g * 8, 8)].reshape(8 * 2 * STRIP, K)
+            sums = jnp.dot(outer, fine, preferred_element_type=f32)
+            yside[m, pl.ds(g * 8, 8)] = sums.reshape(8, 8, K)
         for slot in range(HALF + 4):
-            value = x_sum(lambda x: ysum[m, x, pl.ds(HALF, 8), :], x_cell(slot))
+            value = x_sum(lambda x: yside[m, x], x_cell(slot))
             rows = pl.ds(m * (SLOTS * 8) + slot * 8, 8)
             edge[0, rows, :] = value[:, :LANES]
             edge[1, rows, :] = value[:, LANES:]
@@ -206,15 +236,11 @@
                             h, pl.ds(start, 2), :
                         ]
 
-        if m >= 1:
-            if m == 1:
-                pl.semaphore_wait(barrier, DEEP - 1 + MEMBERS - 1 + 8)
-            for part in (0, 1) if m == 1 else (m,):
-                send(x_out.at[0, part], x_in.at[0, part], (gx_last, gy), 0)
-                send(x_out.at[1, part], x_in.at[1, part], (gx_next, gy), 0)
-                send(y_out.at[0, part], y_in.at[0, part], (gx, gy_last), 1)
-                send(y_out.at[1, part], y_in.at[1, part], (gx, gy_next), 1)
-
+    pl.semaphore_wait(barrier, DEEP - 1 + MEMBERS - 1 + 8)
+    send(x_out.at[0], x_in.at[0], (gx_last, gy), 0)
+    send(x_out.at[1], x_in.at[1], (gx_next, gy), 0)
+    send(y_out.at[0], y_in.at[0], (gx, gy_last), 1)
+    send(y_out.at[1], y_in.at[1], (gx, gy_next), 1)
     for side, oy in ((0, gy_last), (1, gy_next)):
         for other, ox in ((0, gx_last), (1, gx_next)):
             corner = [c_stage[h, side, other] for h in range(2)]
@@ -222,32 +248,29 @@
             send(c_out.at[side, other], c_in.at[side, other], (ox, oy), 2)
 
     along_y = lax.broadcasted_iota(jnp.int32, (16, LANES), 0)
-
-    def inside(step, carry):
-        m = step // 2
-        row = pl.multiple_of(lax.rem(step, 2) * 16, 16)
-        y = along_y + row
-        kept = (y >= 2) & (y < HALF - 2)
-        for h in range(2):
-            lanes = pl.ds(h * LANES, LANES)
-            for cell in range(HALF):
-                value = x_sum(lambda x: ysum[m, x, pl.ds(row, 16), lanes], cell)
-                rows = pl.ds(pl.multiple_of(m * (HALF * HALF) + cell * HALF + row, 16), 16)
-                coarse[h, rows, :] = value
-                rounded[rows, lanes] = jnp.where(kept, value, 0.0).astype(bf16)
-        return carry
-
-    lax.fori_loop(0, PARTS * 2, inside, 0)
-
     blocks[...] = jnp.zeros(blocks.shape, f32)
-    size = (HALF - 4) * HALF // 2
-
-    def cross_inside(step, carry):
-        start = (step // 2) * HALF * HALF + 2 * HALF + lax.rem(step, 2) * size
-        blocks[...] += cross_blocks(rounded[pl.ds(pl.multiple_of(start, 64), size), :])
-        return carry
-
-    lax.fori_loop(0, PARTS * 2, cross_inside, 0)
+    for m in range(PARTS):
+        for q in range(2):
+            loads[m * 2 + q].wait()
+            for g in range(slabs // GROUP):
+                y_pass(m, GROUP + q * slabs + g * GROUP)
+
+        def inside(step, carry, m=m):
+            row = pl.multiple_of(step * 16, 16)
+            y = along_y + row
+            kept = (y >= 2) & (y < HALF - 2)
+            for h in range(2):
+                lanes = pl.ds(h * LANES, LANES)
+                for cell in range(HALF):
+                    value = x_sum(lambda x: ysum[m, x, pl.ds(row, 16), lanes], cell)
+                    rows = pl.ds(pl.multiple_of(m * (HALF * HALF) + cell * HALF + row, 16), 16)
+                    coarse[h, rows, :] = value
+                    rounded[rows, lanes] = jnp.where(kept, value, 0.0).astype(bf16)
+            return carry
+
+        lax.fori_loop(0, 2, inside, 0)
+        rows = pl.ds(m * HALF * HALF + 2 * HALF, (HALF - 4) * HALF)
+        blocks[...] += cross_blocks(rounded[rows, :])
 
     for kind, arrived in enumerate((x_in, y_in, c_in)):
         arrivals(arrived, halo_recv.at[kind])
@@ -390,7 +413,9 @@
         out_specs=(pl.BlockSpec(memory_space=pl.ANY), pl.BlockSpec(memory_space=pltpu.VMEM)),
         scratch_shapes=[
             vmem((PARTS, FINE, FINE, K), bf16),
-            vmem((PARTS, FINE, ROWS, K), f32),
+            vmem((PARTS, FINE, 2 * STRIP, K), bf16),
+            vmem((PARTS, FINE, HALF, K), f32),
+            vmem((PARTS, FINE, 8, K), f32),
             vmem((2, PARTS * SLOTS * 8, LANES), f32),
             vmem((2, rows, LANES), f32),
             vmem((rows, K), bf16),
@@ -407,7 +432,7 @@
             vmem((MEMBERS, 9, LANES), f32),
             vmem((DEEP, 9, LANES), f32),
             vmem((MEMBERS, 9, LANES), f32),
-            dma((PARTS * 2,)),
+            dma((2 + PARTS * 2,)),
             dma,
             dma((3,)),
             dma((3,)),
@@ -428,7 +453,7 @@
     return high, middle, (rest - middle.astype(f32)).astype(bf16)
 
 
-def factor_panels(work, upper, inverse):
+def factor_panels(work, upper, inverse, beside):
     place = lax.broadcasted_iota(jnp.int32, (8, LANES), 0)
     parts = PANEL // 8
     contract = (((0,), (0,)), ((), ()))
@@ -468,9 +493,11 @@
             if j == 2 and later is not None:
                 later()
                 later = None
+            if j == 6 and first >= LANES:
+                beside((first - LANES) // PANEL)
             over = 1.0 / pivot
-            beside = spread(column[(j + 1) // 8], (j + 1) % 8)
-            pivot = spread(columns[j + 1][(j + 1) // 8], (j + 1) % 8) - (beside * beside) * over
+            nearby = spread(column[(j + 1) // 8], (j + 1) % 8)
+            pivot = spread(columns[j + 1][(j + 1) // 8], (j + 1) % 8) - (nearby * nearby) * over
             factor = {}
             for t in range(top if row < 7 else top + 1, parts):
                 value = column[t] * over
@@ -520,39 +547,69 @@
     load.start()
     row = lax.broadcasted_iota(jnp.int32, (K, K), 0)
     column = lax.broadcasted_iota(jnp.int32, (K, K), 1)
-    prior_gram = lax.dot_general(
-        prior_ref[...],
-        prior_ref[...],
-        (((0,), (0,)), ((), ())),
-        precision=lax.Precision.HIGHEST,
-        preferred_element_type=f32,
-    )
+
+    def exact(left, right):
+        return lax.dot_general(
+            left,
+            right,
+            (((0,), (0,)), ((), ())),
+            precision=lax.Precision.HIGHEST,
+            preferred_element_type=f32,
+        )
+
+    prior_top = exact(prior_ref[:LANES, :LANES], prior_ref[:LANES, :])
+    prior_low = exact(prior_ref[:, LANES:], prior_ref[:, LANES:])
     shared = gram_ref[LANES:K, :]
     turned = shared.T
     upper_half = row[:LANES, :LANES] <= column[:LANES, :LANES]
     equal = row[:LANES, :LANES] == column[:LANES, :LANES]
-    work[:LANES, :LANES] = jnp.where(upper_half, shared, turned) + prior_gram[:LANES, :LANES]
-    work[:LANES, LANES:K] = gram_ref[:LANES, :] + prior_gram[:LANES, LANES:]
+    work[:LANES, :LANES] = jnp.where(upper_half, shared, turned) + prior_top[:, :LANES]
+    work[:LANES, LANES:K] = gram_ref[:LANES, :] + prior_top[:, LANES:]
     work[LANES:, :LANES] = jnp.zeros((LANES, LANES), f32)
     work[LANES:, LANES:K] = (
         jnp.where(equal, gram_ref[K : K + 1, :], jnp.where(upper_half, turned, shared))
-        + prior_gram[LANES:, LANES:]
+        + prior_low
     )
     work[:, K:] = jnp.where(row == column, 1.0, 0.0)
-    factor_panels(work, upper, inverse)
-    upper_ref[...] = jnp.where(row <= column, upper[...], 0.0)
-    high, middle, low = split(inverse[...].T)
-    load.wait()
     count = rows_in.shape[0]
-    block = 512
-    for step in range(count // block):
-        rows = pl.ds(step * block, block)
+    block = count // 4
+
+    def give(half, rows):
+        return pltpu.make_async_copy(
+            out.at[half, rows], modes_ref.at[rows, pl.ds(half * LANES, LANES)], store_sem.at[half]
+        )
+
+    def halves(value):
+        great, middle, _ = split(value)
+        return jnp.concatenate([great, middle], axis=0)
+
+    quarter = []
+
+    def first_lanes(q):
+        if q == 0:
+            load.wait()
+            quarter.append(halves(inverse[:LANES, :LANES].T))
+        rows = pl.ds(q * block, block)
+        part = rows_in[rows, :LANES]
+        part = jnp.concatenate([part, part], axis=1)
+        out[0, rows, :] = jnp.dot(part, quarter[0], preferred_element_type=f32)
+        give(0, rows).start()
+
+    factor_panels(work, upper, inverse, first_lanes)
+    rest = halves(inverse[LANES:, :].T)
+    for q in range(4):
+        rows = pl.ds(q * block, block)
         part = rows_in[rows, :]
-        value = jnp.dot(part, high, preferred_element_type=f32)
-        value += jnp.dot(part, middle, preferred_element_type=f32)
-        out[rows, :] = value
-        pltpu.make_async_copy(out.at[rows], modes_ref.at[rows], store_sem).start()
-    pltpu.make_async_copy(out, modes_ref, store_sem).wait()
+        part = jnp.concatenate([part, part], axis=1)
+        out[1, rows, :] = jnp.dot(part, rest, preferred_element_type=f32)
+        give(1, rows).start()
+        if q == 0:
+            upper[...] = jnp.where(row <= column, upper[...], 0.0)
+            store_upper = pltpu.make_async_copy(upper, upper_ref, store_sem.at[2])
+            store_upper.start()
+    store_upper.wait()
+    for half in range(2):
+        give(half, pl.ds(0, count)).wait()
 
 
 def factor_call(coarse, gram, prior):
@@ -562,15 +619,15 @@
         factor_kernel,
         out_shape=(jax.ShapeDtypeStruct((rows, K), f32), jax.ShapeDtypeStruct((K, K), f32)),
         in_specs=[pl.BlockSpec(memory_space=pl.ANY)] + [pl.BlockSpec(memory_space=pltpu.VMEM)] * 2,
-        out_specs=(pl.BlockSpec(memory_space=pl.ANY), pl.BlockSpec(memory_space=pltpu.VMEM)),
+        out_specs=(pl.BlockSpec(memory_space=pl.ANY), pl.BlockSpec(memory_space=pl.ANY)),
         scratch_shapes=[
             vmem((rows, K), bf16),
             vmem((K, 2 * K), f32),
             vmem((K, K), f32),
             vmem((K, K), f32),
-            vmem((rows, K), f32),
+            vmem((2, rows, LANES), f32),
             pltpu.SemaphoreType.DMA,
-            pltpu.SemaphoreType.DMA,
+            pltpu.SemaphoreType.DMA((3,)),
         ],
         compiler_params=pltpu.CompilerParams(vmem_limit_bytes=48 * 2**20),
         name="factor_and_modes",

time: 43.9 us -> 42.9 us (0.977)
  Pallas kernels: 43.2 us -> 42.1 us
    pallas_call x1, Pallas kernels: 10.1 us -> 9.06 us  [factor_call(): pl.pallas_call(factor_kernel, out_shape=(jax.ShapeDtypeStruct((rows, K),...]
where the time goes in v4:
time: 42.9 us; the launch traced here: 42.8 us
  Pallas kernels  42.1 us (98%)
  between operations  0.65 us (2%)
    pallas_call x1, Pallas kernels, filter_call(): pl.pallas_call(filter_kernel, out_shape=(jax.ShapeDtypeStruct((rows, K),...  33.1 us
    pallas_call x1, Pallas kernels, factor_call(): pl.pallas_call(factor_kernel, out_shape=(jax.ShapeDtypeStruct((rows, K),...  9.06 us

profile of v4, /device:TPU:1, one launch (start us, length us, event | category | flops | bytes accessed | tf_op | source)
XLA Modules:
  0.0 42.8 jit_solution(11741750283357086882)
XLA Ops:
  0.6 0.0 copy-start
  0.6 33.1 %filter_and_gram.1 = (bf16[3072,256]{1,0:T(8,128)(2,1)S(1)}, f32[264,128]{1,0:T(8,128)S(1)}) custom-call(bf16[3,64,64,256]{3,2,1,0:T(8,128)(2,1)} %snap_ref.1), custom_call_target="tpu_custom_call" | custom-call | tf_op jit(solution)/shard_map/filter_and_gram/pallas_call | solution.py:406
  33.7 0.0 copy-done
  33.7 9.1 %factor_and_modes.1 = (f32[3072,256]{1,0:T(8,128)}, f32[256,256]{1,0:T(8,128)}) custom-call(bf16[3072,256]{1,0:T(8,128)(2,1)S(1)} %get-tuple-element.6.coarse_ref, f32[264,128]{1,0:T(8,128)S(1)} %get-tuple-element.7.gram_ref, f32[256,256]{1,0:T(8,128)S(1)} %copy-done), custom_call_target="tpu_custom_call" | custom-call | tf_op jit(solution)/shard_map/factor_and_modes/pallas_call | solution.py:618
Async XLA Ops:
  0.6 33.1 %copy-start = (f32[256,256]{1,0:T(8,128)S(1)}, f32[256,256]{1,0:T(8,128)}, u32[]{:S(2)}) copy-start(f32[256,256]{1,0:T(8,128)} %prior_ref.1) | copy-start | bytes 786436

commit v5 on v4

--- a/solution.py
+++ b/solution.py
@@ -142,12 +142,13 @@
     for first in (0, FINE - GROUP):
         place = (slice(None), pl.ds(first, GROUP))
         pltpu.make_async_copy(snap_ref.at[place], tile.at[place], load_sem.at[0]).start()
-    for side in range(2):
-        pltpu.make_async_copy(
-            snap_ref.at[:, :, pl.ds(side * (FINE - STRIP), STRIP)],
-            strip.at[:, :, pl.ds(side * STRIP, STRIP)],
-            load_sem.at[1],
-        ).start()
+    for m in range(PARTS):
+        for side in range(2):
+            pltpu.make_async_copy(
+                snap_ref.at[m, :, pl.ds(side * (FINE - STRIP), STRIP)],
+                strip.at[m, :, pl.ds(side * STRIP, STRIP)],
+                load_sem.at[1 + m],
+            ).start()
     slabs = (FINE - 2 * GROUP) // 2
     loads = []
     for m in range(PARTS):
@@ -155,11 +156,9 @@
             place = (m, pl.ds(GROUP + q * slabs, slabs))
             loads.append(
                 pltpu.make_async_copy(
-                    snap_ref.at[place], tile.at[place], load_sem.at[2 + len(loads)]
+                    snap_ref.at[place], tile.at[place], load_sem.at[1 + PARTS + len(loads)]
                 )
             )
-    for load in loads:
-        load.start()
 
     barrier = pltpu.get_barrier_semaphore()
 
@@ -202,6 +201,8 @@
         ysum[m, pl.ds(first, GROUP)] = sums.reshape(GROUP, HALF, K)
 
     arrivals(tile.at[:, pl.ds(0, 2 * GROUP)], load_sem.at[0])
+    loads[0].start()
+    loads[1].start()
     for m in range(PARTS):
         y_pass(m, 0)
         y_pass(m, FINE - GROUP)
@@ -212,8 +213,11 @@
                 x_out[side, m, step] = value.astype(bf16)
 
     outer = outside_taps()
-    arrivals(strip, load_sem.at[1])
-    for m in range(PARTS):
+    for m in range(PARTS):
+        arrivals(strip.at[m], load_sem.at[1 + m])
+        if m + 1 < PARTS:
+            loads[2 * m + 2].start()
+            loads[2 * m + 3].start()
         for g in range(FINE // 8):
             fine = strip[m, pl.ds(g * 8, 8)].reshape(8 * 2 * STRIP, K)
             sums = jnp.dot(outer, fine, preferred_element_type=f32)
@@ -317,9 +321,7 @@
                 border[place, pl.ds(h * LANES, LANES)] = coarse[h, rows, :].astype(bf16)
 
     total = blocks[...]
-    half_border = PARTS * 4 * HALF
-    for part in range(2):
-        total += cross_blocks(border[pl.ds(part * half_border, half_border), :])
+    total += cross_blocks(border[...])
     mixed, shared, diagonal = pack(total[0], total[1], total[2])
     packed[0 : LANES // 8, 0:8, :] = mixed.reshape(LANES // 8, 8, LANES)
     packed[LANES // 8 :, 0:8, :] = shared.reshape(LANES // 8, 8, LANES)
@@ -432,7 +434,7 @@
             vmem((MEMBERS, 9, LANES), f32),
             vmem((DEEP, 9, LANES), f32),
             vmem((MEMBERS, 9, LANES), f32),
-            dma((2 + PARTS * 2,)),
+            dma((1 + PARTS * 3,)),
             dma,
             dma((3,)),
             dma((3,)),

time: 42.9 us -> 42.9 us (level)
  no operation moved by 1% of the time
where the time goes in v5:
time: 42.9 us; the launch traced here: 42.8 us
  Pallas kernels  42.1 us (98%)
  between operations  0.65 us (2%)
    pallas_call x1, Pallas kernels, filter_call(): pl.pallas_call(filter_kernel, out_shape=(jax.ShapeDtypeStruct((rows, K),...  33.1 us
    pallas_call x1, Pallas kernels, factor_call(): pl.pallas_call(factor_kernel, out_shape=(jax.ShapeDtypeStruct((rows, K),...  9.06 us

profile of v5, /device:TPU:1, one launch (start us, length us, event | category | flops | bytes accessed | tf_op | source)
XLA Modules:
  0.0 42.8 jit_solution(15710194045995265125)
XLA Ops:
  0.6 0.0 copy-start
  0.6 33.1 %filter_and_gram.1 = (bf16[3072,256]{1,0:T(8,128)(2,1)S(1)}, f32[264,128]{1,0:T(8,128)S(1)}) custom-call(bf16[3,64,64,256]{3,2,1,0:T(8,128)(2,1)} %snap_ref.1), custom_call_target="tpu_custom_call" | custom-call | tf_op jit(solution)/shard_map/filter_and_gram/pallas_call | solution.py:408
  33.7 0.0 copy-done
  33.7 9.1 %factor_and_modes.1 = (f32[3072,256]{1,0:T(8,128)}, f32[256,256]{1,0:T(8,128)}) custom-call(bf16[3072,256]{1,0:T(8,128)(2,1)S(1)} %get-tuple-element.6.coarse_ref, f32[264,128]{1,0:T(8,128)S(1)} %get-tuple-element.7.gram_ref, f32[256,256]{1,0:T(8,128)S(1)} %copy-done), custom_call_target="tpu_custom_call" | custom-call | tf_op jit(solution)/shard_map/factor_and_modes/pallas_call | solution.py:620
Async XLA Ops:
  0.6 33.1 %copy-start = (f32[256,256]{1,0:T(8,128)S(1)}, f32[256,256]{1,0:T(8,128)}, u32[]{:S(2)}) copy-start(f32[256,256]{1,0:T(8,128)} %prior_ref.1) | copy-start | bytes 786436

commit v6 on v4

--- a/solution.py
+++ b/solution.py
@@ -24,6 +24,10 @@
 DEEP = 8
 MEMBERS = 32
 PANEL = 32
+OFFSETS = sorted(
+    ((dx, dy, dc) for dx in range(SIDE) for dy in range(SIDE) for dc in range(2) if dx + dy + dc),
+    key=lambda d: -(min(d[0], SIDE - d[0]) + min(d[1], SIDE - d[1])),
+)
 
 
 def tap_matrix(row_slab, cell, column_slab, y, used):
@@ -166,17 +170,16 @@
     def greet(peer):
         pl.semaphore_signal(barrier, inc=1, device_id=peer, device_id_type=MESH)
 
-    def greet_z(step, carry):
-        greet((gx, 2 * lax.rem(zed + step, DEEP) + core))
-        return carry
-
-    def greet_member(step, carry):
-        other = lax.rem(gx * 2 + core + step, MEMBERS)
-        greet((other // 2, 2 * zed + lax.rem(other, 2)))
-        return carry
-
-    lax.fori_loop(1, DEEP, greet_z, 0)
-    lax.fori_loop(1, MEMBERS, greet_member, 0)
+    at_x, at_y = gx // SIDE, lax.rem(gx, SIDE)
+    xs = [SIDE * lax.rem(at_x + d, SIDE) for d in range(SIDE)]
+    ys = [lax.rem(at_y + d, SIDE) for d in range(SIDE)]
+    cores = [core, 1 - core]
+    depths = [2 * lax.rem(zed + d, DEEP) + core for d in (4, 3, 5, 2, 6, 1, 7)]
+
+    for depth in depths:
+        greet((gx, depth))
+    for dx, dy, dc in OFFSETS:
+        greet((xs[dx] + ys[dy], 2 * zed + cores[dc]))
     for oy in (gy_last, gy_next):
         for ox in (gx_last, gx, gx_next):
             greet((ox, oy))
@@ -327,27 +330,17 @@
 
     me = gx * 2 + core
 
-    at_x, at_y = gx // SIDE, lax.rem(gx, SIDE)
-
     def to_members(source_of, target, phase):
-        for far in range(SIDE, -1, -1):
-            for dx in range(SIDE):
-                for dy in range(SIDE):
-                    if min(dx, SIDE - dx) + min(dy, SIDE - dy) != far:
-                        continue
-                    peer = SIDE * lax.rem(at_x + dx, SIDE) + lax.rem(at_y + dy, SIDE)
-                    for dc in range(2):
-                        if dx + dy + dc == 0:
-                            continue
-                        there = lax.rem(core + dc, 2)
-                        pltpu.make_async_remote_copy(
-                            src_ref=source_of(peer * 2 + there),
-                            dst_ref=target.at[me],
-                            send_sem=sum_send.at[phase],
-                            recv_sem=sum_recv.at[phase],
-                            device_id=(peer, 2 * zed + there),
-                            device_id_type=MESH,
-                        ).start()
+        for dx, dy, dc in OFFSETS:
+            peer = xs[dx] + ys[dy]
+            pltpu.make_async_remote_copy(
+                src_ref=source_of(peer * 2 + cores[dc]),
+                dst_ref=target.at[me],
+                send_sem=sum_send.at[phase],
+                recv_sem=sum_recv.at[phase],
+                device_id=(peer, 2 * zed + cores[dc]),
+                device_id_type=MESH,
+            ).start()
 
     def sum_slots(slots, count):
         total = slots[0]
@@ -372,13 +365,13 @@
     arrivals(rs_in.at[pl.ds(0, MEMBERS - 1)], sum_recv.at[0])
 
     z_in[zed] = sum_slots(rs_in, MEMBERS)
-    for step in (4, 3, 5, 2, 6, 1, 7):
+    for depth in depths:
         pltpu.make_async_remote_copy(
             src_ref=z_in.at[zed],
             dst_ref=z_in.at[zed],
             send_sem=sum_send.at[1],
             recv_sem=sum_recv.at[1],
-            device_id=(gx, 2 * lax.rem(zed + step, DEEP) + core),
+            device_id=(gx, depth),
             device_id_type=MESH,
         ).start()
     arrivals(z_in.at[pl.ds(0, DEEP - 1)], sum_recv.at[1])

time: 42.9 us -> 42.3 us (0.986)
  Pallas kernels: 42.1 us -> 41.6 us
    pallas_call x1, Pallas kernels: 33.1 us -> 32.5 us  [filter_call(): pl.pallas_call(filter_kernel, out_shape=(jax.ShapeDtypeStruct((rows, K),...]
where the time goes in v6:
time: 42.3 us; the launch traced here: 42.2 us
  Pallas kernels  41.6 us (98%)
  between operations  0.65 us (2%)
    pallas_call x1, Pallas kernels, filter_call(): pl.pallas_call(filter_kernel, out_shape=(jax.ShapeDtypeStruct((rows, K),...  32.5 us
    pallas_call x1, Pallas kernels, factor_call(): pl.pallas_call(factor_kernel, out_shape=(jax.ShapeDtypeStruct((rows, K),...  9.06 us

profile of v6, /device:TPU:1, one launch (start us, length us, event | category | flops | bytes accessed | tf_op | source)
XLA Modules:
  0.0 42.2 jit_solution(11774860682329259499)
XLA Ops:
  0.6 0.0 copy-start
  0.6 32.5 %filter_and_gram.1 = (bf16[3072,256]{1,0:T(8,128)(2,1)S(1)}, f32[264,128]{1,0:T(8,128)S(1)}) custom-call(bf16[3,64,64,256]{3,2,1,0:T(8,128)(2,1)} %snap_ref.1), custom_call_target="tpu_custom_call" | custom-call | tf_op jit(solution)/shard_map/filter_and_gram/pallas_call | solution.py:399
  33.2 0.0 copy-done
  33.2 9.1 %factor_and_modes.1 = (f32[3072,256]{1,0:T(8,128)}, f32[256,256]{1,0:T(8,128)}) custom-call(bf16[3072,256]{1,0:T(8,128)(2,1)S(1)} %get-tuple-element.6.coarse_ref, f32[264,128]{1,0:T(8,128)S(1)} %get-tuple-element.7.gram_ref, f32[256,256]{1,0:T(8,128)S(1)} %copy-done), custom_call_target="tpu_custom_call" | custom-call | tf_op jit(solution)/shard_map/factor_and_modes/pallas_call | solution.py:611
Async XLA Ops:
  0.6 32.5 %copy-start = (f32[256,256]{1,0:T(8,128)S(1)}, f32[256,256]{1,0:T(8,128)}, u32[]{:S(2)}) copy-start(f32[256,256]{1,0:T(8,128)} %prior_ref.1) | copy-start | bytes 786436
